TPU v7x, 256 devices: a whole 4x4x8 slice. The times are simulated.
256 devices in a mesh: gz: 256 (over y, x, z, core).
Axes of the slice: x: 4, y: 4, z: 8, core: 2. Of those that a mesh axis runs over, the one named last changes fastest.
Arguments:
- tokens: bfloat16 [256, 64, 128, 128], P('gz'), may hold values from -64 to 64
- cotangent: bfloat16 [256, 64, 128, 128], P('gz'), may hold values from -24 to 24
- w_query: bfloat16 [128, 128], replicated, may hold values from -1 to 1
- w_key: bfloat16 [128, 128], replicated, may hold values from -0.5 to 0.5
- w_value: bfloat16 [128, 128], replicated, may hold values from -0.5 to 0.5
- w_out: bfloat16 [128, 128], replicated, may hold values from -0.5 to 0.5
- ln_gain: float32 [128], replicated, may hold values from 0.5 to 1.5
- ln_bias: float32 [128], replicated, may hold values from -1 to 1
Outputs:
- d_tokens: bfloat16 [256, 64, 128, 128], P('gz')
- d_query: float32 [128, 128], replicated
- d_out: float32 [128, 128], replicated
- d_key: float32 [128, 128], replicated
- d_value: float32 [128, 128], replicated
- d_gain: float32 [128], replicated
- d_bias: float32 [128], replicated
- pooled_grad: float32 [512, 128], replicated
All inputs are finite; a program needn't handle non-finite values.
Results may differ from a plain program's by a relative error of at most 0.023.
The roundings to bfloat16 on the way count: a program that leaves them out, or rounds other values in their place, can miss the bound.
Values sent between devices are 32-bit elements; how exact they have to be, the bound alone decides.
A program may use at most 64 MiB of HBM per device.

v0:
```python
import jax
import jax.numpy as jnp
from jax import lax
from jax.sharding import PartitionSpec as P

HEADS = 4
POOL = 16


EPSILON = 1e-05


def layer_norm_rows(pooled, ln_gain, ln_bias):
    row_mean = jnp.mean(pooled, axis=1, keepdims=True)
    centered = pooled - row_mean
    row_var = jnp.mean(centered * centered, axis=1, keepdims=True)
    inv_std = lax.rsqrt(row_var + EPSILON)
    standard = centered * inv_std
    return (standard, inv_std, standard * ln_gain + ln_bias)


def key_backward(key_grads, value_grads, standard, inv_std, normed_low, w_key, w_value, ln_gain):
    normed_wide = normed_low.astype(jnp.float32)
    grad_key = jnp.einsum("kd,ke->de", normed_wide, key_grads, precision=lax.Precision.HIGHEST)
    grad_value = jnp.einsum("kd,ke->de", normed_wide, value_grads, precision=lax.Precision.HIGHEST)
    key_low = key_grads.astype(jnp.bfloat16)
    value_low = value_grads.astype(jnp.bfloat16)
    d_normed = jnp.dot(key_low, w_key.T, preferred_element_type=jnp.float32) + jnp.dot(
        value_low, w_value.T, preferred_element_type=jnp.float32
    )
    grad_gain = jnp.sum(d_normed * standard, axis=0)
    grad_bias = jnp.sum(d_normed, axis=0)
    scaled = d_normed * ln_gain
    d_pooled = inv_std * (
        scaled
        - jnp.mean(scaled, axis=1, keepdims=True)
        - standard * jnp.mean(scaled * standard, axis=1, keepdims=True)
    )
    return (d_pooled, grad_key, grad_value, grad_gain, grad_bias)


def body(tokens, cotangent, w_query, w_key, w_value, w_out, ln_gain, ln_bias):
    devices = lax.axis_size("gz")
    device_index = lax.axis_index("gz")
    rows_y, plane_x, features = (tokens.shape[1], tokens.shape[2], tokens.shape[3])
    cells_y = rows_y // POOL
    cells_x = plane_x // POOL
    cells_dev = cells_y * cells_x
    key_count = cells_dev * devices // POOL
    head_dim = features // HEADS
    score_scale = head_dim ** (-0.5)
    slab_rows = rows_y * plane_x
    slab_tokens = tokens[0]
    partial_value = jnp.sum(
        slab_tokens.astype(jnp.float32).reshape(cells_y, POOL, cells_x, POOL, features), axis=(1, 3)
    ).reshape(cells_dev, features)
    offset = (device_index // (2 * POOL) * 2 + device_index % 2) * cells_dev
    placed = lax.dynamic_update_slice(
        jnp.zeros((key_count, features), jnp.float32), partial_value, (offset, 0)
    )
    pooled = lax.psum(placed, "gz") / float(POOL**3)
    standard, inv_std, normed = layer_norm_rows(pooled, ln_gain, ln_bias)
    normed_low = normed.astype(jnp.bfloat16)
    key_rows = jnp.dot(normed_low, w_key, preferred_element_type=jnp.float32).astype(jnp.bfloat16)
    value_rows = jnp.dot(normed_low, w_value, preferred_element_type=jnp.float32).astype(
        jnp.bfloat16
    )
    key_heads = key_rows.reshape(key_count, HEADS, head_dim)
    value_heads = value_rows.reshape(key_count, HEADS, head_dim)
    block_rows = min(512, slab_rows)
    block_count = slab_rows // block_rows
    query_blocks = slab_tokens.reshape(block_count, block_rows, features)
    grad_blocks = cotangent[0].reshape(block_count, block_rows, features)

    def per_block(running, inputs):
        query_rows, grad_rows = inputs
        query_low = jnp.dot(query_rows, w_query, preferred_element_type=jnp.float32).astype(
            jnp.bfloat16
        )
        query_heads = query_low.reshape(block_rows, HEADS, head_dim)
        scores = (
            jnp.einsum("qhe,khe->hqk", query_heads, key_heads, preferred_element_type=jnp.float32)
            * score_scale
        )
        row_max = jnp.max(scores, axis=2, keepdims=True)
        exponent = jnp.exp(scores - row_max)
        attention = exponent / jnp.sum(exponent, axis=2, keepdims=True)
        attention_low = attention.astype(jnp.bfloat16)
        attn_low = (
            jnp.einsum(
                "hqk,khe->qhe", attention_low, value_heads, preferred_element_type=jnp.float32
            )
            .reshape(block_rows, features)
            .astype(jnp.bfloat16)
        )
        out_part = jnp.einsum("qd,qe->de", attn_low, grad_rows, preferred_element_type=jnp.float32)
        d_attn_low = jnp.dot(grad_rows, w_out.T, preferred_element_type=jnp.float32).astype(
            jnp.bfloat16
        )
        d_heads = d_attn_low.reshape(block_rows, HEADS, head_dim)
        d_probs = jnp.einsum(
            "qhe,khe->hqk", d_heads, value_heads, preferred_element_type=jnp.float32
        )
        row_delta = jnp.sum(attention * d_probs, axis=2, keepdims=True)
        d_scores_low = (attention * (d_probs - row_delta) * score_scale).astype(jnp.bfloat16)
        value_part = jnp.einsum(
            "hqk,qhe->khe", attention_low, d_heads, preferred_element_type=jnp.float32
        )
        key_part = jnp.einsum(
            "hqk,qhe->khe", d_scores_low, query_heads, preferred_element_type=jnp.float32
        )
        dq_low = (
            jnp.einsum("hqk,khe->qhe", d_scores_low, key_heads, preferred_element_type=jnp.float32)
            .reshape(block_rows, features)
            .astype(jnp.bfloat16)
        )
        query_part = jnp.einsum("qd,qe->de", query_rows, dq_low, preferred_element_type=jnp.float32)
        return (
            (
                running[0] + key_part,
                running[1] + value_part,
                running[2] + query_part,
                running[3] + out_part,
            ),
            dq_low,
        )

    zero_keys = jnp.zeros((key_count, HEADS, head_dim), jnp.float32)
    zero_square = jnp.zeros((features, features), jnp.float32)
    totals, dq_blocks = lax.scan(
        per_block, (zero_keys, zero_keys, zero_square, zero_square), (query_blocks, grad_blocks)
    )
    dq_all = dq_blocks.reshape(slab_rows, features)
    query_input_grad = jnp.dot(dq_all, w_query.T, preferred_element_type=jnp.float32)
    key_partial = totals[0].reshape(key_count, features)
    value_partial = totals[1].reshape(key_count, features)
    share_rows = key_count // devices
    share_start = device_index * share_rows
    key_share, value_share = (
        lax.psum_scatter(key_partial, "gz", scatter_dimension=0, tiled=True),
        lax.psum_scatter(value_partial, "gz", scatter_dimension=0, tiled=True),
    )
    standard_share = lax.dynamic_slice_in_dim(standard, share_start, share_rows, 0)
    inv_share = lax.dynamic_slice_in_dim(inv_std, share_start, share_rows, 0)
    normed_share = lax.dynamic_slice_in_dim(normed_low, share_start, share_rows, 0)
    pooled_share, key_piece, value_piece, gain_piece, bias_piece = key_backward(
        key_share, value_share, standard_share, inv_share, normed_share, w_key, w_value, ln_gain
    )
    d_pooled = lax.all_gather(pooled_share, "gz", axis=0, tiled=True)
    grad_query, grad_out, grad_key, grad_value, grad_gain, grad_bias = lax.psum(
        (totals[2], totals[3], key_piece, value_piece, gain_piece, bias_piece), "gz"
    )
    own_rows = lax.dynamic_slice_in_dim(d_pooled, offset, cells_dev, 0) / float(POOL**3)
    spread = jnp.broadcast_to(
        own_rows.reshape(cells_y, 1, cells_x, 1, features), (cells_y, POOL, cells_x, POOL, features)
    ).reshape(slab_rows, features)
    d_tokens = (
        (query_input_grad + spread).astype(jnp.bfloat16).reshape(1, rows_y, plane_x, features)
    )
    grad_scale = float(devices * slab_rows) ** (-0.5)
    return (
        d_tokens,
        grad_query * grad_scale,
        grad_out * grad_scale,
        grad_key * grad_scale,
        grad_value * grad_scale,
        grad_gain * grad_scale,
        grad_bias * grad_scale,
        d_pooled * grad_scale,
    )


def solution(mesh):
    in_specs = (P("gz", None, None, None), P("gz", None, None, None), P(), P(), P(), P(), P(), P())
    out_specs = (P("gz", None, None, None), P(), P(), P(), P(), P(), P(), P())
    return jax.shard_map(body, mesh=mesh, in_specs=in_specs, out_specs=out_specs, check_vma=False)
```

profile of v0, /device:TPU:1, one launch (start us, length us, event | category | flops | bytes accessed | tf_op | source)
XLA Modules:
  0.0 1438.3 jit_solution(1005434058069082377)
XLA Ops:
  10.1 256.6 %all-reduce.9.cloned.1.call-done = f32[512,128]{1,0:T(8,128)} async-done(((f32[512,128]{1,0:T(8,128)}), f32[512,128]{1,0:T(8,128)}) %all-reduce.9.cloned.1.call-update) | async-done | bytes 262160 | tf_op jit(solution)/shard_map/psum | solution.py:61
  271.5 513.2 %while.19 = (s32[]{:T(128)}, f32[512,4,32]{0,2,1:T(8,128)S(1)}, f32[512,4,32]{0,2,1:T(8,128)}, f32[128,128]{1,0:T(8,128)S(1)}, f32[128,128]{1,0:T(8,128)S(1)}, /...) while((s32[]{:T(128)}, f32[512,4,32]{0,2,1:T(8,128)S(1)}, ...), condition=%wide.region_8.9_spmd.clone, body=%wide.region_4.8_spmd.clone.sunk | while | flops 492377600 | bytes 37855404 | solution.py:130
  279.9 7.3 fusion.129
  290.8 7.6 fusion.131
  322.9 7.6 fusion.131
  344.0 7.3 fusion.129
  355.0 7.6 fusion.131
  387.1 7.6 fusion.131
  419.2 7.6 fusion.131
  451.2 7.6 fusion.131
  483.3 7.6 fusion.131
  515.4 7.6 fusion.131
  547.5 7.6 fusion.131
  579.5 7.6 fusion.131
  611.6 7.6 fusion.131
  643.7 7.6 fusion.131
  675.8 7.6 fusion.131
  707.8 7.6 fusion.131
  739.9 7.6 fusion.131
  772.0 7.6 fusion.131
  785.5 251.0 %all-reduce.13.cloned.1.call-done = (f32[512,128]{0,1:T(8,128)}, f32[512,128]{0,1:T(8,128)}) async-done(((f32[512,128]{0,1:T(8,128)}, f32[512,128]{0,1:T(8,128)}), (f32[512,128]{0,1:T(8,128)}, f32[512,128]{0,1:T(8,128)})) %all-reduce.13.cloned.1.call-update) | async-done | bytes 524304
  1042.5 62.5 %all-gather = f32[256,2,128]{2,1,0:T(2,128)S(1)} all-gather(f32[1,2,128]{2,1,0:T(2,128)S(1)} %multiply_bitcast_fusion.1), channel_id=1, replica_groups=mesh['gz'=256] {'gz'}, dimensions={0}, use_global_device_ids=true | all-gather | bytes 263168 | tf_op jit(solution)/shard_map/all_gather | solution.py:149
  1108.2 74.6 %all-reduce.2 = (f32[128]{0:T(128)S(1)}, f32[128]{0:T(128)S(1)}) all-reduce(f32[128]{0:T(128)S(1)} %get-tuple-element.118, f32[128]{0:T(128)S(1)} %get-tuple-element.121), channel_id=1, replica_groups=mesh['gz'=256] {'gz'}, use_global_device_ids=true, to_apply=%region_18.19 | all-reduce | flops 256 | bytes 2048 | tf_op jit(solution)/shard_map/psum | solution.py:150
  1183.4 245.4 %all-reduce.11.cloned.1.call-done = (f32[128,128]{1,0:T(8,128)}, f32[128,128]{1,0:T(8,128)}, f32[128,128]{1,0:T(8,128)}, f32[128,128]{1,0:T(8,128)}) async-done(((f32[128,128]{1,0:T(8,128)}, f32[128,128]{1,0:T(8,128)}, f32[128,128]{1,0:T(8,128)}, f32[128,128]{1,0:T(8,128)}), (f32[128,128]{1,0:T(8,128)}, f32[128,128]{1,0:T(8,128)}, f32[128,128]{1,0:T(8,128)}, ...) | async-done | bytes 262160 | tf_op jit(solution)/shard_map/psum | solution.py:150
  (227 shorter events, 396.7 us)
Async XLA Ops:
  7.2 264.0 %copy-start = (bf16[128,128]{1,0:T(8,128)(2,1)S(1)}, bf16[128,128]{1,0:T(8,128)(2,1)}, u32[]{:S(2)}) copy-start(bf16[128,128]{1,0:T(8,128)(2,1)} %param.14) | copy-start | bytes 98308
  7.2 264.3 %copy-start.3 = (bf16[128,128]{1,0:T(8,128)(2,1)S(1)}, bf16[128,128]{1,0:T(8,128)(2,1)}, u32[]{:S(2)}) copy-start(bf16[128,128]{1,0:T(8,128)(2,1)} %param.12) | copy-start | bytes 98308
  7.2 264.3 %copy-start.5 = (bf16[128,128]{1,0:T(8,128)(2,1)S(1)}, bf16[128,128]{1,0:T(8,128)(2,1)}, u32[]{:S(2)}) copy-start(bf16[128,128]{1,0:T(8,128)(2,1)} %param.15) | copy-start | bytes 98308
  7.2 259.5 %all-reduce.9.cloned.1.call-start = ((), (), s32[]{:S(2)}) async-start(), calls=%async_computation | async-start | bytes 524288 | tf_op jit(solution)/shard_map/psum | solution.py:61
  9.3 0.7 copy-start.4
  10.0 1026.5 %all-reduce.13.cloned.1.call-start = ((), (), s32[]{:S(2)}) async-start(), calls=%async_computation.2 | async-start | bytes 1048576
  271.5 765.1 %copy-start.7 = (bf16[128,128]{1,0:T(8,128)(2,1)S(1)}, bf16[128,128]{1,0:T(8,128)(2,1)}, u32[]{:S(2)}) copy-start(bf16[128,128]{1,0:T(8,128)(2,1)} %param.13) | copy-start | bytes 98308
  271.5 769.7 %copy-start.8 = (f32[128]{0:T(128)S(1)}, f32[128]{0:T(128)}, u32[]{:S(2)}) copy-start(f32[128]{0:T(128)} %param.16) | copy-start | bytes 1540
  784.7 0.7 copy-start.6
  784.7 323.5 %copy-start.1 = (f32[128,128]{1,0:T(8,128)}, f32[128,128]{1,0:T(8,128)S(1)}, u32[]{:S(2)}) copy-start(f32[128,128]{1,0:T(8,128)S(1)} %get-tuple-element.77) | copy-start | bytes 196612
  784.7 323.5 %copy-start.2 = (f32[128,128]{1,0:T(8,128)}, f32[128,128]{1,0:T(8,128)S(1)}, u32[]{:S(2)}) copy-start(f32[128,128]{1,0:T(8,128)S(1)} %get-tuple-element.78) | copy-start | bytes 196612
  785.4 643.3 %all-reduce.11.cloned.1.call-start = ((), (), s32[]{:S(2)}) async-start(), calls=%async_computation.1 | async-start | bytes 524288 | tf_op jit(solution)/shard_map/psum | solution.py:150
Sparse Core Ops, SparseCore 0:
  14.1 252.6 all-reduce.8
  785.5 250.9 all-reduce.12
  1183.0 245.7 all-reduce.10
where the time goes:
time: 1440 us
  waiting for transfers between devices  753 us (52%)
  matrix products  519 us (36%)
  blocking collectives  137 us (10%)
    psum x1, waiting for transfers between devices, body(): pooled = lax.psum(placed, 'gz') / float(POOL ** 3)  257 us
    unnamed x4, waiting for transfers between devices  251 us
    psum x1, waiting for transfers between devices, body(): lax.psum((totals[2], totals[3], key_piece, value_piece, gain_piece, bias_...  245 us
    dot_general x16, matrix products, per_block(): jnp.einsum('hqk,khe->qhe', d_scores_low, key_heads, preferred_element_typ...  122 us
    dot_general x16, matrix products, per_block(): jnp.einsum('hqk,qhe->khe', d_scores_low, query_heads, preferred_element_t...  117 us
    psum x1, blocking collectives, body(): lax.psum((totals[2], totals[3], key_piece, value_piece, gain_piece, bias_...  74.6 us
    all_gather x1, blocking collectives, body(): d_pooled = lax.all_gather(pooled_share, 'gz', axis=0, tiled=True)  62.5 us
    dot_general x16, matrix products, per_block(): jnp.einsum('hqk,qhe->khe', attention_low, d_heads, preferred_element_type...  58.4 us
  transfers between devices with their start and end apart: 3, of which 3 were waited for; matrix products, arithmetic and copies ran while one was open for 0% of the time, Pallas kernels for 0%

commit v1 on v0

v1 whole, which is shorter than its diff:
```python
import functools
import math

import jax
import jax.numpy as jnp
from jax import lax
from jax.experimental import pallas as pl
from jax.experimental.pallas import tpu as pltpu
from jax.sharding import PartitionSpec as P

HEADS = 4
POOL = 16
EPSILON = 1e-05
MESH = pl.DeviceIdType.MESH
F32 = jnp.float32
BF16 = jnp.bfloat16

Z = 8
PLANE = 16
QUERIES = 256
KEY_CHUNK = 128
SAFE_LOG2 = 60.0


def dot(a, b):
    return lax.dot_general(a, b, (((1,), (0,)), ((), ())), preferred_element_type=F32)


def dot_nt(a, b):
    return lax.dot_general(a, b, (((1,), (1,)), ((), ())), preferred_element_type=F32)


def greet(partners):
    barrier = pltpu.get_barrier_semaphore()
    for partner in partners:
        pl.semaphore_signal(barrier, inc=1, device_id=(partner,), device_id_type=MESH)
    pl.semaphore_wait(barrier, len(partners))


def send(src, dst, send_sem, recv_sem, partner):
    copy = pltpu.make_async_remote_copy(
        src_ref=src,
        dst_ref=dst,
        send_sem=send_sem,
        recv_sem=recv_sem,
        device_id=(partner,),
        device_id_type=MESH,
    )
    copy.start()
    return copy


def pool_kernel(part_ref, out_ref, near, far, near_send, near_recv, far_send, far_recv):
    me = lax.axis_index("gz")
    core, chip = lax.rem(me, 2), me // 2
    member, block = lax.rem(chip, 16), chip // 16
    group = block * 2 + core
    near_ids, far_ids = [], []
    for t in range(1, 16):
        near_ids.append((block * 16 + lax.rem(member + t, 16)) * 2 + core)
        other = lax.rem(group + t, 16)
        far_ids.append(((other // 2) * 16 + member) * 2 + lax.rem(other, 2))
    greet(near_ids + far_ids)
    copies = [
        send(part_ref, near.at[member], near_send.at[t], near_recv.at[t], near_ids[t])
        for t in range(15)
    ]
    near[member] = part_ref[...]
    for copy in copies:
        copy.wait()
    total = near[0]
    for m in range(1, 16):
        total = total + near[m]
    far[group] = total
    copies = [
        send(far.at[group], far.at[group], far_send.at[t], far_recv.at[t], far_ids[t])
        for t in range(15)
    ]
    for copy in copies:
        copy.wait()
    for g in range(16):
        out_ref[pl.ds(g * 32, 32), :] = far[g]


def exchange_pools(part):
    rows, features = part.shape
    return pl.pallas_call(
        pool_kernel,
        name="pool_exchange",
        out_shape=jax.ShapeDtypeStruct((16 * rows, features), F32),
        in_specs=[pl.BlockSpec(memory_space=pltpu.VMEM)],
        out_specs=pl.BlockSpec(memory_space=pltpu.VMEM),
        scratch_shapes=[
            pltpu.VMEM((16, rows, features), F32),
            pltpu.VMEM((16, rows, features), F32),
            pltpu.SemaphoreType.DMA((15,)),
            pltpu.SemaphoreType.DMA((15,)),
            pltpu.SemaphoreType.DMA((15,)),
            pltpu.SemaphoreType.DMA((15,)),
        ],
        compiler_params=pltpu.CompilerParams(collective_id=0, has_side_effects=True),
    )(part)


def sum_kernel(
    w_ref, out_ref, got_half, half, got, along, full, pair_send, pair_recv, sum_send, sum_recv,
    z_send, z_recv, all_send, all_recv,
):
    me = lax.axis_index("gz")
    core, chip = lax.rem(me, 2), me // 2
    z, plane = lax.rem(chip, Z), chip // Z
    half_rows = half.shape[0]
    share = half_rows // PLANE
    sibling = me + 1 - 2 * core
    plane_members = [lax.rem(plane + t, PLANE) for t in range(1, PLANE)]
    plane_ids = [(other * Z + z) * 2 + core for other in plane_members]
    z_ids = [(plane * Z + lax.rem(z + t, Z)) * 2 + core for t in range(1, Z)]
    greet([sibling] + plane_ids + z_ids)

    mine = pl.ds(pl.multiple_of(core * half_rows, 8), half_rows)
    theirs = pl.ds(pl.multiple_of((1 - core) * half_rows, 8), half_rows)
    send(w_ref.at[theirs], got_half, pair_send.at[0], pair_recv.at[0], sibling).wait()
    half[...] = w_ref[mine, :] + got_half[...]

    copies = [
        send(
            half.at[pl.ds(pl.multiple_of(plane_members[t] * share, 8), share)],
            got.at[t],
            sum_send.at[t],
            sum_recv.at[t],
            plane_ids[t],
        )
        for t in range(PLANE - 1)
    ]
    total = half[pl.ds(pl.multiple_of(plane * share, 8), share), :]
    for t in range(PLANE - 1):
        copies[t].wait()
        total = total + got[t]

    along[z] = total
    copies = [
        send(along.at[z], along.at[z], z_send.at[t], z_recv.at[t], z_ids[t]) for t in range(Z - 1)
    ]
    for copy in copies:
        copy.wait()
    total = along[0]
    for k in range(1, Z):
        total = total + along[k]
    own = pl.ds(pl.multiple_of(core * half_rows + plane * share, 8), share)
    full[own, :] = total

    copies = [
        send(full.at[own], full.at[own], all_send.at[t], all_recv.at[t], plane_ids[t])
        for t in range(PLANE - 1)
    ]
    for copy in copies:
        copy.wait()
    send(full.at[mine], full.at[mine], pair_send.at[1], pair_recv.at[1], sibling).wait()
    out_ref[...] = full[...]


def sum_devices(w):
    rows, features = w.shape
    share = rows // 2 // PLANE
    dma = pltpu.SemaphoreType.DMA
    return pl.pallas_call(
        sum_kernel,
        name="sum_devices",
        out_shape=jax.ShapeDtypeStruct((rows, features), F32),
        in_specs=[pl.BlockSpec(memory_space=pltpu.VMEM)],
        out_specs=pl.BlockSpec(memory_space=pltpu.VMEM),
        scratch_shapes=[
            pltpu.VMEM((rows // 2, features), F32),
            pltpu.VMEM((rows // 2, features), F32),
            pltpu.VMEM((PLANE - 1, share, features), F32),
            pltpu.VMEM((Z, share, features), F32),
            pltpu.VMEM((rows, features), F32),
            dma((2,)),
            dma((2,)),
            dma((PLANE - 1,)),
            dma((PLANE - 1,)),
            dma((Z - 1,)),
            dma((Z - 1,)),
            dma((PLANE - 1,)),
            dma((PLANE - 1,)),
        ],
        compiler_params=pltpu.CompilerParams(collective_id=1, has_side_effects=True),
    )(w)


def normalise(pool_sums):
    pooled = pool_sums * (1.0 / float(POOL**3))
    mean = jnp.mean(pooled, axis=1, keepdims=True)
    centered = pooled - mean
    var = jnp.mean(centered * centered, axis=1, keepdims=True)
    inv_std = lax.rsqrt(var + EPSILON)
    return centered * inv_std, inv_std


def transposed(w):
    return w.astype(F32).T.astype(BF16)


def three_terms(low, factor, lane_group):
    wide = low.astype(F32) * factor
    high = wide.astype(BF16)
    rest = wide - high.astype(F32)
    middle = rest.astype(BF16)
    last = (rest - middle.astype(F32)).astype(BF16)
    zero = jnp.zeros_like(high)
    return jnp.where(
        lane_group == 0,
        high,
        jnp.where(lane_group == 1, middle, jnp.where(lane_group == 2, last, zero)),
    )


def attend_kernel(
    tokens_ref, cot_ref, pool_ref, w_query_ref, w_key_ref, w_value_ref, w_out_ref, gain_ref,
    bias_ref, sums_ref, dq_ref, q_rows, q_cols, d_rows, d_cols, key_terms, value_terms, key_cols,
    value_cols, exps, dps, probs, dscores,
):
    blocks, queries, features = tokens_ref.shape
    keys = pool_ref.shape[0]
    head_dim = features // HEADS
    scale = head_dim ** (-0.5)
    chunks = keys // KEY_CHUNK

    standard, _ = normalise(pool_ref[...])
    normed_low = (standard * gain_ref[...] + bias_ref[...]).astype(BF16)
    source = lax.broadcasted_iota(jnp.int32, (features, HEADS * features), 0)
    target = lax.broadcasted_iota(jnp.int32, (features, HEADS * features), 1)
    spread = jnp.where(
        source == (target // features) * head_dim + lax.rem(target, head_dim), 1.0, 0.0
    ).astype(BF16)
    lane = lax.broadcasted_iota(jnp.int32, (keys, features), 1)
    lane_group = lane // head_dim
    for w_ref, factor, terms, cols in (
        (w_key_ref, scale * math.log2(math.e), key_terms, key_cols),
        (w_value_ref, scale, value_terms, value_cols),
    ):
        w = w_ref[...]
        wide_w = dot(w, spread).astype(BF16)
        for h in range(HEADS):
            low = dot(normed_low, wide_w[:, h * features : (h + 1) * features]).astype(BF16)
            terms[h] = three_terms(low, factor, lane_group)
        cols[...] = dot_nt(transposed(w), normed_low).astype(BF16)
    key_wide = key_cols[...].astype(F32).reshape(HEADS, head_dim, keys)
    key_norm = jnp.max(jnp.sum(key_wide * key_wide, axis=1), axis=1, keepdims=True)

    w_query = w_query_ref[...]
    w_query_t = transposed(w_query)
    w_out = w_out_ref[...]
    w_out_t = transposed(w_out)

    def project(i, norm):
        rows, grads = tokens_ref[i], cot_ref[i]
        q_rows[i] = dot(rows, w_query).astype(BF16)
        d_rows[i] = dot(grads, w_out_t).astype(BF16)
        cols = dot_nt(w_query_t, rows).astype(BF16)
        q_cols[i] = cols
        d_cols[i] = dot_nt(w_out, grads).astype(BF16)
        wide = cols.astype(F32).reshape(HEADS, head_dim, queries)
        return jnp.maximum(norm, jnp.sum(wide * wide, axis=1))

    norm = lax.fori_loop(0, blocks, project, jnp.zeros((HEADS, queries), F32))
    bound = jnp.max(norm * key_norm) * (scale * math.log2(math.e)) ** 2

    sums_ref[...] = jnp.zeros_like(sums_ref)
    query_head = lax.broadcasted_iota(jnp.int32, (queries, features), 1) // head_dim

    def fold(x):
        return jnp.sum(x.reshape(x.shape[0] // 8, 8, queries), axis=0)

    def first(i, h, slot, safe):
        query = q_cols[i, h * head_dim : (h + 1) * head_dim, :]
        grad = d_cols[i, h * head_dim : (h + 1) * head_dim, :]
        query = jnp.concatenate([query] * HEADS, axis=0)
        grad = jnp.concatenate([grad] * HEADS, axis=0)
        total = jnp.zeros((8, queries), F32)
        delta = jnp.zeros((8, queries), F32)
        if safe:
            top = jnp.full((8, queries), -jnp.inf, F32)
            for c in range(chunks):
                part = pl.ds(c * KEY_CHUNK, KEY_CHUNK)
                s = dot(key_terms[h, part, :], query)
                exps[slot, part, :] = s
                top = jnp.maximum(
                    top, jnp.max(s.reshape(KEY_CHUNK // 8, 8, queries), axis=0)
                )
            top = jnp.max(top, axis=0, keepdims=True)
        for c in range(chunks):
            part = pl.ds(c * KEY_CHUNK, KEY_CHUNK)
            if safe:
                e = jnp.exp2(exps[slot, part, :] - top)
            else:
                e = jnp.exp2(dot(key_terms[h, part, :], query))
            dp = dot(value_terms[h, part, :], grad)
            exps[slot, part, :] = e
            dps[slot, part, :] = dp
            total = total + fold(e)
            delta = delta + fold(e * dp)
        return total, delta

    def second(h, slot, bank, sums):
        total, delta = (jnp.sum(x, axis=0, keepdims=True) for x in sums)
        inverse = 1.0 / total
        delta = delta * inverse
        columns = pl.ds(h * queries, queries)
        for c in range(chunks):
            part = pl.ds(c * KEY_CHUNK, KEY_CHUNK)
            p = exps[slot, part, :] * inverse
            probs[bank, part, columns] = p.astype(BF16)
            dscores[bank, part, columns] = (p * (dps[slot, part, :] - delta)).astype(BF16)
        head = pl.ds(h * head_dim, head_dim)
        attn = dot(value_cols[head, :], probs[bank, :, columns])
        dq = dot(key_cols[head, :], dscores[bank, :, columns])
        return attn, dq

    def third(i, bank, outs):
        attn_low = jnp.concatenate([o[0] for o in outs], axis=0).astype(BF16)
        dq_low = jnp.concatenate([o[1] for o in outs], axis=0).astype(BF16)
        sums_ref[pl.ds(2 * keys, features), :] += dot(dq_low, tokens_ref[i])
        sums_ref[pl.ds(2 * keys + features, features), :] += dot(attn_low, cot_ref[i])
        dq_ref[i] = dq_low.astype(F32).T.astype(BF16)
        zero = jnp.zeros((queries, features), BF16)
        q, d = q_rows[i], d_rows[i]
        q_stack = jnp.concatenate([jnp.where(query_head == h, q, zero) for h in range(HEADS)], 0)
        d_stack = jnp.concatenate([jnp.where(query_head == h, d, zero) for h in range(HEADS)], 0)
        sums_ref[pl.ds(0, keys), :] += dot(dscores[bank], q_stack)
        sums_ref[pl.ds(keys, keys), :] += dot(probs[bank], d_stack)

    def run(at_once, safe):
        def step(j, carry):
            units = [(b, h) for b in range(at_once) for h in range(HEADS)]
            pending = first(j * at_once, 0, 0, safe)
            outs = []
            for n, (b, h) in enumerate(units):
                current = pending
                if n + 1 < len(units):
                    nb, nh = units[n + 1]
                    pending = first(j * at_once + nb, nh, (n + 1) % 2, safe)
                outs.append(second(h, n % 2, b, current))
                if h == HEADS - 1:
                    third(j * at_once + b, b, outs)
                    outs = []
            return carry

        lax.fori_loop(0, blocks // at_once, step, 0)

    @pl.when(bound <= SAFE_LOG2**2)
    def _():
        run(2, False)

    @pl.when(jnp.logical_not(bound <= SAFE_LOG2**2))
    def _():
        run(1, True)


def attend(tokens, cot, pool_sums, w_query, w_key, w_value, w_out, gain, bias):
    blocks, queries, features = tokens.shape
    keys = pool_sums.shape[0]
    flops = 2 * blocks * queries * features * (6 * keys + 6 * features)
    vmem = pl.BlockSpec(memory_space=pltpu.VMEM)
    return pl.pallas_call(
        attend_kernel,
        name="attend",
        out_shape=(
            jax.ShapeDtypeStruct((2 * keys + 2 * features, features), F32),
            jax.ShapeDtypeStruct((blocks, queries, features), BF16),
        ),
        in_specs=[vmem] * 9,
        out_specs=(vmem, vmem),
        scratch_shapes=[
            pltpu.VMEM((blocks, queries, features), BF16),
            pltpu.VMEM((blocks, features, queries), BF16),
            pltpu.VMEM((blocks, queries, features), BF16),
            pltpu.VMEM((blocks, features, queries), BF16),
            pltpu.VMEM((HEADS, keys, features), BF16),
            pltpu.VMEM((HEADS, keys, features), BF16),
            pltpu.VMEM((features, keys), BF16),
            pltpu.VMEM((features, keys), BF16),
            pltpu.VMEM((2, keys, queries), F32),
            pltpu.VMEM((2, keys, queries), F32),
            pltpu.VMEM((2, keys, HEADS * queries), BF16),
            pltpu.VMEM((2, keys, HEADS * queries), BF16),
        ],
        cost_estimate=pl.CostEstimate(
            flops=flops,
            bytes_accessed=3 * tokens.size * 2,
            transcendentals=blocks * queries * keys * HEADS,
        ),
        compiler_params=pltpu.CompilerParams(vmem_limit_bytes=48 * 1024 * 1024),
    )(tokens, cot, pool_sums, w_query, w_key, w_value, w_out, gain, bias)


def split_dot(low, wide):
    turned = low.astype(F32).T.astype(BF16)
    high = wide.astype(BF16)
    rest = wide - high.astype(F32)
    middle = rest.astype(BF16)
    last = (rest - middle.astype(F32)).astype(BF16)
    return dot(turned, high) + dot(turned, middle) + dot(turned, last)


def finish_kernel(
    grad_scale, sums_ref, pool_ref, dq_ref, w_query_ref, w_key_ref, w_value_ref, gain_ref,
    bias_ref, d_tokens_ref, d_query_ref, d_out_ref, d_key_ref, d_value_ref, d_gain_ref,
    d_bias_ref, pooled_grad_ref, own,
):
    keys, features = pool_ref.shape
    step = pl.program_id(0)
    cells_y, cells_x = 4, 8
    cells = cells_y * cells_x

    @pl.when(step == 0)
    def _():
        standard, inv_std = normalise(pool_ref[...])
        gain = gain_ref[...]
        normed_low = (standard * gain + bias_ref[...]).astype(BF16)
        key_grads = sums_ref[pl.ds(0, keys), :]
        value_grads = sums_ref[pl.ds(keys, keys), :]
        d_key_ref[...] = split_dot(normed_low, key_grads) * grad_scale
        d_value_ref[...] = split_dot(normed_low, value_grads) * grad_scale
        d_normed = dot_nt(key_grads.astype(BF16), w_key_ref[...]) + dot_nt(
            value_grads.astype(BF16), w_value_ref[...]
        )
        d_gain_ref[...] = jnp.sum(d_normed * standard, axis=0, keepdims=True) * grad_scale
        d_bias_ref[...] = jnp.sum(d_normed, axis=0, keepdims=True) * grad_scale
        scaled = d_normed * gain
        d_pooled = inv_std * (
            scaled
            - jnp.mean(scaled, axis=1, keepdims=True)
            - standard * jnp.mean(scaled * standard, axis=1, keepdims=True)
        )
        pooled_grad_ref[...] = d_pooled * grad_scale
        own[...] = d_pooled * (1.0 / float(POOL**3))
        d_query_ref[...] = sums_ref[pl.ds(2 * keys, features), :].T * grad_scale
        d_out_ref[...] = sums_ref[pl.ds(2 * keys + features, features), :] * grad_scale

    rows = dq_ref.shape[0]
    plane_x = cells_x * POOL
    me = lax.axis_index("gz")
    offset = (me // (2 * POOL) * 2 + lax.rem(me, 2)) * cells
    cell_y = step * rows // (plane_x * POOL)
    mine = own[pl.ds(pl.multiple_of(offset + cell_y * cells_x, 8), cells_x), :]
    spread = jnp.concatenate(
        [jnp.broadcast_to(mine[x : x + 1, :], (POOL, features)) for x in range(cells_x)], axis=0
    )
    product = dot_nt(dq_ref[...], w_query_ref[...])
    summed = product.reshape(rows // plane_x, plane_x, features) + spread[None]
    d_tokens_ref[...] = summed.reshape(rows, features).astype(BF16)


def finish(sums, pool_sums, dq, w_query, w_key, w_value, gain, bias, grad_scale):
    keys, features = pool_sums.shape
    tokens = dq.shape[0]
    rows = 1024

    def whole(*shape):
        return pl.BlockSpec(shape, lambda i: (0,) * len(shape))

    square = whole(features, features)
    line = whole(1, features)
    tile = pl.BlockSpec((rows, features), lambda i: (i, 0))
    return pl.pallas_call(
        functools.partial(finish_kernel, grad_scale),
        name="finish",
        grid=(tokens // rows,),
        out_shape=(
            jax.ShapeDtypeStruct((tokens, features), BF16),
            *[jax.ShapeDtypeStruct((features, features), F32)] * 4,
            *[jax.ShapeDtypeStruct((1, features), F32)] * 2,
            jax.ShapeDtypeStruct((keys, features), F32),
        ),
        in_specs=[
            whole(*sums.shape), whole(keys, features), tile, square, square, square, line, line,
        ],
        out_specs=(tile, square, square, square, square, line, line, whole(keys, features)),
        scratch_shapes=[pltpu.VMEM((keys, features), F32)],
        compiler_params=pltpu.CompilerParams(vmem_limit_bytes=32 * 1024 * 1024),
    )(sums, pool_sums, dq, w_query, w_key, w_value, gain, bias)


def body(tokens, cotangent, w_query, w_key, w_value, w_out, ln_gain, ln_bias):
    devices = lax.axis_size("gz")
    _, rows_y, plane_x, features = tokens.shape
    cells_y, cells_x = rows_y // POOL, plane_x // POOL
    slab_rows = rows_y * plane_x
    part = jnp.sum(
        tokens.astype(F32).reshape(cells_y, POOL, cells_x, POOL, features), axis=(1, 3)
    ).reshape(cells_y * cells_x, features)
    pool_sums = exchange_pools(part)
    gain, bias = ln_gain.reshape(1, features), ln_bias.reshape(1, features)
    blocks = slab_rows // QUERIES
    sums, dq = attend(
        tokens.reshape(blocks, QUERIES, features),
        cotangent.reshape(blocks, QUERIES, features),
        pool_sums, w_query, w_key, w_value, w_out, gain, bias,
    )
    sums = sum_devices(sums)
    grad_scale = float(devices * slab_rows) ** (-0.5)
    d_tokens, d_query, d_out, d_key, d_value, d_gain, d_bias, pooled_grad = finish(
        sums, pool_sums, dq.reshape(slab_rows, features), w_query, w_key, w_value, gain, bias,
        grad_scale,
    )
    return (
        d_tokens.reshape(1, rows_y, plane_x, features),
        d_query,
        d_out,
        d_key,
        d_value,
        d_gain.reshape(features),
        d_bias.reshape(features),
        pooled_grad,
    )


def solution(mesh):
    in_specs = (P("gz", None, None, None), P("gz", None, None, None), P(), P(), P(), P(), P(), P())
    out_specs = (P("gz", None, None, None), P(), P(), P(), P(), P(), P(), P())
    return jax.shard_map(body, mesh=mesh, in_specs=in_specs, out_specs=out_specs, check_vma=False)
```

time: 1440 us -> 150 us (0.10)
  waiting for transfers between devices: 753 us -> 0 us
  matrix products: 519 us -> 0 us
  Pallas kernels: 0 us -> 140 us
  blocking collectives: 137 us -> 0 us
    psum x2 -> x0, waiting for transfers between devices: 502 us -> none  [the longest x1 257 us: body(): pooled = lax.psum(placed, 'gz') / float(POOL ** 3)]
    dot_general x151 -> x0, matrix products: 463 us -> none  [the longest x16 122 us: per_block(): jnp.einsum('hqk,khe->qhe', d_scores_low, key_heads, preferred_element_typ...]
    unnamed x4 -> x0, waiting for transfers between devices: 251 us -> none
    pallas_call x0 -> x4, Pallas kernels: none -> 140 us  [the longest x1 80.9 us: attend(): pl.pallas_call(attend_kernel, name='attend', out_shape=(jax.ShapeDtypeStr...]
    psum x1 -> x0, blocking collectives: 74.6 us -> none  [body(): lax.psum((totals[2], totals[3], key_piece, value_piece, gain_piece, bias_...]
    all_gather x1 -> x0, blocking collectives: 62.5 us -> none  [body(): d_pooled = lax.all_gather(pooled_share, 'gz', axis=0, tiled=True)]
    sub x16 -> x0, matrix products: 55.5 us -> none  [per_block(): exponent = jnp.exp(scores - row_max)]
  transfers between devices with their start and end apart: 3 -> 0, of which waited for: 3 -> 0; matrix products, arithmetic and copies ran while one was open for 0% -> 0% of each run, Pallas kernels for 0% -> 0%
where the time goes in v1:
time: 150 us
  Pallas kernels  140 us (93%)
  local copies, waits for them, and re-layouts  5.82 us (4%)
  other arithmetic  2.71 us (2%)
    pallas_call x1, Pallas kernels, attend(): pl.pallas_call(attend_kernel, name='attend', out_shape=(jax.ShapeDtypeStr...  80.9 us
    pallas_call x1, Pallas kernels, sum_devices(): pl.pallas_call(sum_kernel, name='sum_devices', out_shape=jax.ShapeDtypeSt...  28.5 us
    pallas_call x1, Pallas kernels, exchange_pools(): pl.pallas_call(pool_kernel, name='pool_exchange', out_shape=jax.ShapeDtyp...  26 us
    unnamed x26, local copies, waits for them, and re-layouts  5.82 us
    pallas_call x1, Pallas kernels, finish(): pl.pallas_call(functools.partial(finish_kernel, grad_scale), name='finish...  4.89 us

profile of v1, /device:TPU:1, one launch (start us, length us, event | category | flops | bytes accessed | tf_op | source)
XLA Modules:
  0.0 149.6 jit_solution(1041434838593462212)
XLA Ops:
  0.6 0.0 copy-start.9
  0.6 0.0 copy-start.8
  0.7 0.0 copy-start.7
  0.7 0.0 copy-start.1
  0.7 0.0 copy-start.11
  0.7 0.0 copy-start.10
  0.7 0.0 copy-start.12
  0.7 2.7 %convert_reduce_fusion = f32[4,8,128]{2,1,0:T(8,128)} fusion(bf16[4,16,8,16,128]{4,3,2,1,0:T(8,128)(2,1)} %bitcast.11), kind=kLoop, calls=%fused_computation | loop fusion | flops 2093056 | bytes 2113536 | tf_op jit(solution)/shard_map/reduce_sum | solution.py:490
  3.4 26.0 %pool_exchange.1.pool_ref = f32[512,128]{1,0:T(8,128)} custom-call(f32[32,128]{1,0:T(8,128)} %bitcast.18), custom_call_target="tpu_custom_call" | custom-call | tf_op jit(solution)/shard_map/pool_exchange/pallas_call | solution.py:87
  29.4 0.0 copy-done.9
  29.4 0.0 copy-done.8
  29.4 0.0 copy-done.7
  29.4 0.0 copy-done.1
  29.5 0.9 copy-done.4
  30.4 80.9 %attend.1 = (f32[1280,128]{1,0:T(8,128)S(1)}, bf16[32,256,128]{2,1,0:T(8,128)(2,1)S(1)}) custom-call(bf16[32,256,128]{2,1,0:T(8,128)(2,1)S(1)} %bitcast.12, bf16[32,256,128]{2,1,0:T(8,128)(2,1)} %bitcast.19, f32[512,128]{1,0:T(8,128)S(1)} %copy-done.4, bf16[128,128]{1,0:T(8,128)(2,1)S(1)} %copy-done.7, bf16[128,128]{1,0:T(8,128)(2,1)S(1)} %copy-done.8, ...), custom_call_target="tpu_custom_call" | custom-call | flops 8053063680 | bytes 6291456 | tf_op jit(solution)/shard_map/attend/pallas_call | solution.py:365
  111.3 0.0 copy-start.2
  111.4 1.3 copy-done.2
  112.7 0.9 copy-done.6
  113.5 28.5 %sum_devices.1.sums_ref = f32[1280,128]{1,0:T(8,128)} custom-call(f32[1280,128]{1,0:T(8,128)} %copy-done.6), custom_call_target="tpu_custom_call" | custom-call | tf_op jit(solution)/shard_map/sum_devices/pallas_call | solution.py:166
  142.1 0.0 copy-done.5
  142.1 0.0 copy-start
  142.1 1.1 copy-done
  143.2 1.6 %copy-done.3 = bf16[32,256,128]{2,1,0:T(8,128)(2,1)S(1)} copy-done((bf16[32,256,128]{2,1,0:T(8,128)(2,1)S(1)}, bf16[32,256,128]{2,1,0:T(8,128)(2,1)}, u32[]{:S(2)}) %copy-start.3) | copy-done | bytes 2097176
  144.7 4.9 %finish.1 = (bf16[8192,128]{1,0:T(8,128)(2,1)}, f32[128,128]{1,0:T(8,128)}, f32[128,128]{1,0:T(8,128)}, f32[128,128]{1,0:T(8,128)}, f32[128,128]{1,0:T(8,128)}, ...) custom-call(f32[1280,128]{1,0:T(8,128)S(1)} %copy-done, f32[512,128]{1,0:T(8,128)S(1)} %copy-done.5, ...), custom_call_target="tpu_custom_call" | custom-call | tf_op jit(solution)/shard_map/finish/pallas_call | solution.py:466
  (7 shorter events, 0.0 us)
Async XLA Ops:
  0.6 28.8 %copy-start.9 = (bf16[128,128]{1,0:T(8,128)(2,1)S(1)}, bf16[128,128]{1,0:T(8,128)(2,1)}, u32[]{:S(2)}) copy-start(bf16[128,128]{1,0:T(8,128)(2,1)} %w_value_ref.3) | copy-start | bytes 98308
  0.6 28.8 %copy-start.8 = (bf16[128,128]{1,0:T(8,128)(2,1)S(1)}, bf16[128,128]{1,0:T(8,128)(2,1)}, u32[]{:S(2)}) copy-start(bf16[128,128]{1,0:T(8,128)(2,1)} %w_key_ref.3) | copy-start | bytes 98308
  0.7 28.8 %copy-start.7 = (bf16[128,128]{1,0:T(8,128)(2,1)S(1)}, bf16[128,128]{1,0:T(8,128)(2,1)}, u32[]{:S(2)}) copy-start(bf16[128,128]{1,0:T(8,128)(2,1)} %w_query_ref.3) | copy-start | bytes 98308
  0.7 28.8 %copy-start.1 = (bf16[1,64,128,128]{3,2,1,0:T(8,128)(2,1)S(1)}, bf16[1,64,128,128]{3,2,1,0:T(8,128)(2,1)}, u32[]{:S(2)}) copy-start(bf16[1,64,128,128]{3,2,1,0:T(8,128)(2,1)} %param.8) | copy-start | bytes 6291460
  0.7 28.8 %copy-start.11 = (f32[128]{0:T(128)S(1)}, f32[128]{0:T(128)}, u32[]{:S(2)}) copy-start(f32[128]{0:T(128)} %param.15) | copy-start | bytes 1540
  0.7 28.8 %copy-start.10 = (f32[128]{0:T(128)S(1)}, f32[128]{0:T(128)}, u32[]{:S(2)}) copy-start(f32[128]{0:T(128)} %param.14) | copy-start | bytes 1540
  0.7 28.8 %copy-start.12 = (bf16[128,128]{1,0:T(8,128)(2,1)S(1)}, bf16[128,128]{1,0:T(8,128)(2,1)}, u32[]{:S(2)}) copy-start(bf16[128,128]{1,0:T(8,128)(2,1)} %w_out_ref.1) | copy-start | bytes 98308
  29.5 1.0 copy-start.4
  30.4 111.6 %copy-start.5 = (f32[512,128]{1,0:T(8,128)S(1)}, f32[512,128]{1,0:T(8,128)}, u32[]{:S(2)}) copy-start(f32[512,128]{1,0:T(8,128)} %pool_exchange.1.pool_ref) | copy-start | bytes 786436
  111.3 1.3 copy-start.2
  112.7 0.9 copy-start.6
  142.1 1.1 copy-start
  143.2 1.6 %copy-start.3 = (bf16[32,256,128]{2,1,0:T(8,128)(2,1)S(1)}, bf16[32,256,128]{2,1,0:T(8,128)(2,1)}, u32[]{:S(2)}) copy-start(bf16[32,256,128]{2,1,0:T(8,128)(2,1)} %copy-done.2) | copy-start | bytes 6291460

commit v2 on v1

--- a/solution.py
+++ b/solution.py
@@ -34,7 +34,7 @@
     barrier = pltpu.get_barrier_semaphore()
     for partner in partners:
         pl.semaphore_signal(barrier, inc=1, device_id=(partner,), device_id_type=MESH)
-    pl.semaphore_wait(barrier, len(partners))
+    return lambda: pl.semaphore_wait(barrier, len(partners))
 
 
 def send(src, dst, send_sem, recv_sem, partner):
@@ -50,28 +50,50 @@
     return copy
 
 
-def pool_kernel(part_ref, out_ref, near, far, near_send, near_recv, far_send, far_recv):
+def pool_kernel(
+    tokens_ref, out_ref, pieces, got, near, far, sum_send, sum_recv, near_send, near_recv,
+    far_send, far_recv,
+):
+    cells_y, _, plane_x, features = tokens_ref.shape
+    cells_x = plane_x // POOL
     me = lax.axis_index("gz")
     core, chip = lax.rem(me, 2), me // 2
     member, block = lax.rem(chip, 16), chip // 16
     group = block * 2 + core
-    near_ids, far_ids = [], []
+    members = [lax.rem(member + t, 16) for t in range(1, 16)]
+    near_ids = [(block * 16 + other) * 2 + core for other in members]
+    far_ids = []
     for t in range(1, 16):
-        near_ids.append((block * 16 + lax.rem(member + t, 16)) * 2 + core)
         other = lax.rem(group + t, 16)
         far_ids.append(((other // 2) * 16 + member) * 2 + lax.rem(other, 2))
-    greet(near_ids + far_ids)
+    await_partners = greet(near_ids + far_ids)
+
+    share = got.shape[1]
+    for y in range(cells_y):
+        rows = jnp.sum(tokens_ref[y].astype(F32), axis=0)
+        cells = jnp.sum(rows.reshape(cells_x, POOL, features), axis=1)
+        for x in range(cells_x // share):
+            pieces[y * (cells_x // share) + x] = cells[x * share : (x + 1) * share, :]
+    await_partners()
     copies = [
-        send(part_ref, near.at[member], near_send.at[t], near_recv.at[t], near_ids[t])
+        send(pieces.at[members[t]], got.at[t], sum_send.at[t], sum_recv.at[t], near_ids[t])
         for t in range(15)
     ]
-    near[member] = part_ref[...]
+    total = pieces[member]
+    for t in range(15):
+        copies[t].wait()
+        total = total + got[t]
+
+    near[member] = total
+    copies = [
+        send(near.at[member], near.at[member], near_send.at[t], near_recv.at[t], near_ids[t])
+        for t in range(15)
+    ]
     for copy in copies:
         copy.wait()
-    total = near[0]
-    for m in range(1, 16):
-        total = total + near[m]
-    far[group] = total
+    for m in range(16):
+        far[group, pl.ds(m * share, share), :] = near[m]
+
     copies = [
         send(far.at[group], far.at[group], far_send.at[t], far_recv.at[t], far_ids[t])
         for t in range(15)
@@ -82,8 +104,10 @@
         out_ref[pl.ds(g * 32, 32), :] = far[g]
 
 
-def exchange_pools(part):
-    rows, features = part.shape
+def exchange_pools(tokens):
+    cells_y, _, plane_x, features = tokens.shape
+    rows = cells_y * (plane_x // POOL)
+    dma = pltpu.SemaphoreType.DMA
     return pl.pallas_call(
         pool_kernel,
         name="pool_exchange",
@@ -91,101 +115,140 @@
         in_specs=[pl.BlockSpec(memory_space=pltpu.VMEM)],
         out_specs=pl.BlockSpec(memory_space=pltpu.VMEM),
         scratch_shapes=[
+            pltpu.VMEM((16, rows // 16, features), F32),
+            pltpu.VMEM((15, rows // 16, features), F32),
+            pltpu.VMEM((16, rows // 16, features), F32),
             pltpu.VMEM((16, rows, features), F32),
-            pltpu.VMEM((16, rows, features), F32),
-            pltpu.SemaphoreType.DMA((15,)),
-            pltpu.SemaphoreType.DMA((15,)),
-            pltpu.SemaphoreType.DMA((15,)),
-            pltpu.SemaphoreType.DMA((15,)),
+            *[dma((15,))] * 6,
         ],
-        compiler_params=pltpu.CompilerParams(collective_id=0, has_side_effects=True),
-    )(part)
+        compiler_params=pltpu.CompilerParams(
+            collective_id=0, has_side_effects=True, vmem_limit_bytes=8 * 1024 * 1024
+        ),
+    )(tokens)
+
+
+STREAMS = ((0, 24), (24, 16))
 
 
 def sum_kernel(
     w_ref, out_ref, got_half, half, got, along, full, pair_send, pair_recv, sum_send, sum_recv,
-    z_send, z_recv, all_send, all_recv,
+    z_send, z_recv, all_send, all_recv, back_send, back_recv,
 ):
     me = lax.axis_index("gz")
     core, chip = lax.rem(me, 2), me // 2
     z, plane = lax.rem(chip, Z), chip // Z
-    half_rows = half.shape[0]
-    share = half_rows // PLANE
     sibling = me + 1 - 2 * core
     plane_members = [lax.rem(plane + t, PLANE) for t in range(1, PLANE)]
     plane_ids = [(other * Z + z) * 2 + core for other in plane_members]
     z_ids = [(plane * Z + lax.rem(z + t, Z)) * 2 + core for t in range(1, Z)]
-    greet([sibling] + plane_ids + z_ids)
-
-    mine = pl.ds(pl.multiple_of(core * half_rows, 8), half_rows)
-    theirs = pl.ds(pl.multiple_of((1 - core) * half_rows, 8), half_rows)
-    send(w_ref.at[theirs], got_half, pair_send.at[0], pair_recv.at[0], sibling).wait()
-    half[...] = w_ref[mine, :] + got_half[...]
-
-    copies = [
+    greet([sibling] + plane_ids + z_ids)()
+
+    own = core * PLANE + plane
+    mine = pl.ds(core * PLANE, PLANE)
+    theirs = pl.ds((1 - core) * PLANE, PLANE)
+    streams = range(len(STREAMS))
+    rows = [pl.ds(*stream) for stream in STREAMS]
+
+    pairs = [
         send(
-            half.at[pl.ds(pl.multiple_of(plane_members[t] * share, 8), share)],
-            got.at[t],
-            sum_send.at[t],
-            sum_recv.at[t],
-            plane_ids[t],
-        )
-        for t in range(PLANE - 1)
+            w_ref.at[theirs, rows[s]], got_half.at[:, rows[s]], pair_send.at[s], pair_recv.at[s],
+            sibling,
+        )
+        for s in streams
     ]
-    total = half[pl.ds(pl.multiple_of(plane * share, 8), share), :]
-    for t in range(PLANE - 1):
-        copies[t].wait()
-        total = total + got[t]
-
-    along[z] = total
-    copies = [
-        send(along.at[z], along.at[z], z_send.at[t], z_recv.at[t], z_ids[t]) for t in range(Z - 1)
-    ]
-    for copy in copies:
+    shares = []
+    for s in streams:
+        pairs[s].wait()
+        half[:, rows[s], :] = w_ref[mine, rows[s], :] + got_half[:, rows[s], :]
+        shares.append(
+            [
+                send(
+                    half.at[plane_members[t], rows[s]], got.at[t, rows[s]], sum_send.at[s, t],
+                    sum_recv.at[s, t], plane_ids[t],
+                )
+                for t in range(PLANE - 1)
+            ]
+        )
+    lines = []
+    for s in streams:
+        total = half[plane, rows[s], :]
+        for t in range(PLANE - 1):
+            shares[s][t].wait()
+            total = total + got[t, rows[s], :]
+        along[z, rows[s], :] = total
+        lines.append(
+            [
+                send(
+                    along.at[z, rows[s]], along.at[z, rows[s]], z_send.at[s, t], z_recv.at[s, t],
+                    z_ids[t],
+                )
+                for t in range(Z - 1)
+            ]
+        )
+    gathers = []
+    for s in streams:
+        for copy in lines[s]:
+            copy.wait()
+        total = along[0, rows[s], :]
+        for k in range(1, Z):
+            total = total + along[k, rows[s], :]
+        full[own, rows[s], :] = total
+        gathers.append(
+            [
+                send(
+                    full.at[own, rows[s]], full.at[own, rows[s]], all_send.at[s, t],
+                    all_recv.at[s, t], plane_ids[t],
+                )
+                for t in range(PLANE - 1)
+            ]
+        )
+    backs = []
+    for s in streams:
+        for copy in gathers[s]:
+            copy.wait()
+        backs.append(
+            send(
+                full.at[mine, rows[s]], full.at[mine, rows[s]], back_send.at[s], back_recv.at[s],
+                sibling,
+            )
+        )
+    for copy in backs:
         copy.wait()
-    total = along[0]
-    for k in range(1, Z):
-        total = total + along[k]
-    own = pl.ds(pl.multiple_of(core * half_rows + plane * share, 8), share)
-    full[own, :] = total
-
-    copies = [
-        send(full.at[own], full.at[own], all_send.at[t], all_recv.at[t], plane_ids[t])
-        for t in range(PLANE - 1)
-    ]
-    for copy in copies:
-        copy.wait()
-    send(full.at[mine], full.at[mine], pair_send.at[1], pair_recv.at[1], sibling).wait()
     out_ref[...] = full[...]
 
 
 def sum_devices(w):
     rows, features = w.shape
     share = rows // 2 // PLANE
+    count = len(STREAMS)
     dma = pltpu.SemaphoreType.DMA
     return pl.pallas_call(
         sum_kernel,
         name="sum_devices",
-        out_shape=jax.ShapeDtypeStruct((rows, features), F32),
+        out_shape=jax.ShapeDtypeStruct((2 * PLANE, share, features), F32),
         in_specs=[pl.BlockSpec(memory_space=pltpu.VMEM)],
         out_specs=pl.BlockSpec(memory_space=pltpu.VMEM),
         scratch_shapes=[
-            pltpu.VMEM((rows // 2, features), F32),
-            pltpu.VMEM((rows // 2, features), F32),
+            pltpu.VMEM((PLANE, share, features), F32),
+            pltpu.VMEM((PLANE, share, features), F32),
             pltpu.VMEM((PLANE - 1, share, features), F32),
             pltpu.VMEM((Z, share, features), F32),
-            pltpu.VMEM((rows, features), F32),
-            dma((2,)),
-            dma((2,)),
-            dma((PLANE - 1,)),
-            dma((PLANE - 1,)),
-            dma((Z - 1,)),
-            dma((Z - 1,)),
-            dma((PLANE - 1,)),
-            dma((PLANE - 1,)),
+            pltpu.VMEM((2 * PLANE, share, features), F32),
+            dma((count,)),
+            dma((count,)),
+            dma((count, PLANE - 1)),
+            dma((count, PLANE - 1)),
+            dma((count, Z - 1)),
+            dma((count, Z - 1)),
+            dma((count, PLANE - 1)),
+            dma((count, PLANE - 1)),
+            dma((count,)),
+            dma((count,)),
         ],
-        compiler_params=pltpu.CompilerParams(collective_id=1, has_side_effects=True),
-    )(w)
+        compiler_params=pltpu.CompilerParams(
+            collective_id=1, has_side_effects=True, vmem_limit_bytes=10 * 1024 * 1024
+        ),
+    )(w.reshape(2 * PLANE, share, features)).reshape(rows, features)
 
 
 def normalise(pool_sums):
@@ -218,7 +281,7 @@
 def attend_kernel(
     tokens_ref, cot_ref, pool_ref, w_query_ref, w_key_ref, w_value_ref, w_out_ref, gain_ref,
     bias_ref, sums_ref, dq_ref, q_rows, q_cols, d_rows, d_cols, key_terms, value_terms, key_cols,
-    value_cols, exps, dps, probs, dscores,
+    value_cols, exps, dps, probs, dscores, key_sums, value_sums,
 ):
     blocks, queries, features = tokens_ref.shape
     keys = pool_ref.shape[0]
@@ -267,8 +330,8 @@
     bound = jnp.max(norm * key_norm) * (scale * math.log2(math.e)) ** 2
 
     sums_ref[...] = jnp.zeros_like(sums_ref)
-    query_head = lax.broadcasted_iota(jnp.int32, (queries, features), 1) // head_dim
-
+    key_sums[...] = jnp.zeros_like(key_sums)
+    value_sums[...] = jnp.zeros_like(value_sums)
     def fold(x):
         return jnp.sum(x.reshape(x.shape[0] // 8, 8, queries), axis=0)
 
@@ -279,23 +342,14 @@
         grad = jnp.concatenate([grad] * HEADS, axis=0)
         total = jnp.zeros((8, queries), F32)
         delta = jnp.zeros((8, queries), F32)
+        scores = dot(key_terms[h], query)
+        d_probs = dot(value_terms[h], grad)
         if safe:
-            top = jnp.full((8, queries), -jnp.inf, F32)
-            for c in range(chunks):
-                part = pl.ds(c * KEY_CHUNK, KEY_CHUNK)
-                s = dot(key_terms[h, part, :], query)
-                exps[slot, part, :] = s
-                top = jnp.maximum(
-                    top, jnp.max(s.reshape(KEY_CHUNK // 8, 8, queries), axis=0)
-                )
-            top = jnp.max(top, axis=0, keepdims=True)
+            scores = scores - jnp.max(scores, axis=0, keepdims=True)
         for c in range(chunks):
-            part = pl.ds(c * KEY_CHUNK, KEY_CHUNK)
-            if safe:
-                e = jnp.exp2(exps[slot, part, :] - top)
-            else:
-                e = jnp.exp2(dot(key_terms[h, part, :], query))
-            dp = dot(value_terms[h, part, :], grad)
+            part = slice(c * KEY_CHUNK, (c + 1) * KEY_CHUNK)
+            e = jnp.exp2(scores[part, :])
+            dp = d_probs[part, :]
             exps[slot, part, :] = e
             dps[slot, part, :] = dp
             total = total + fold(e)
@@ -306,15 +360,16 @@
         total, delta = (jnp.sum(x, axis=0, keepdims=True) for x in sums)
         inverse = 1.0 / total
         delta = delta * inverse
-        columns = pl.ds(h * queries, queries)
         for c in range(chunks):
             part = pl.ds(c * KEY_CHUNK, KEY_CHUNK)
+            rows = pl.ds(h * keys + c * KEY_CHUNK, KEY_CHUNK)
             p = exps[slot, part, :] * inverse
-            probs[bank, part, columns] = p.astype(BF16)
-            dscores[bank, part, columns] = (p * (dps[slot, part, :] - delta)).astype(BF16)
+            probs[bank, rows, :] = p.astype(BF16)
+            dscores[bank, rows, :] = (p * (dps[slot, part, :] - delta)).astype(BF16)
         head = pl.ds(h * head_dim, head_dim)
-        attn = dot(value_cols[head, :], probs[bank, :, columns])
-        dq = dot(key_cols[head, :], dscores[bank, :, columns])
+        rows = pl.ds(h * keys, keys)
+        attn = dot(value_cols[head, :], probs[bank, rows, :])
+        dq = dot(key_cols[head, :], dscores[bank, rows, :])
         return attn, dq
 
     def third(i, bank, outs):
@@ -323,12 +378,8 @@
         sums_ref[pl.ds(2 * keys, features), :] += dot(dq_low, tokens_ref[i])
         sums_ref[pl.ds(2 * keys + features, features), :] += dot(attn_low, cot_ref[i])
         dq_ref[i] = dq_low.astype(F32).T.astype(BF16)
-        zero = jnp.zeros((queries, features), BF16)
-        q, d = q_rows[i], d_rows[i]
-        q_stack = jnp.concatenate([jnp.where(query_head == h, q, zero) for h in range(HEADS)], 0)
-        d_stack = jnp.concatenate([jnp.where(query_head == h, d, zero) for h in range(HEADS)], 0)
-        sums_ref[pl.ds(0, keys), :] += dot(dscores[bank], q_stack)
-        sums_ref[pl.ds(keys, keys), :] += dot(probs[bank], d_stack)
+        key_sums[...] += dot(dscores[bank], q_rows[i])
+        value_sums[...] += dot(probs[bank], d_rows[i])
 
     def run(at_once, safe):
         def step(j, carry):
@@ -355,6 +406,12 @@
     @pl.when(jnp.logical_not(bound <= SAFE_LOG2**2))
     def _():
         run(1, True)
+
+    for start, wide in ((0, key_sums), (keys, value_sums)):
+        total = wide[pl.ds(0, keys), :]
+        for h in range(1, HEADS):
+            total = jnp.where(lane_group == h, wide[pl.ds(h * keys, keys), :], total)
+        sums_ref[pl.ds(start, keys), :] = total
 
 
 def attend(tokens, cot, pool_sums, w_query, w_key, w_value, w_out, gain, bias):
@@ -382,15 +439,17 @@
             pltpu.VMEM((features, keys), BF16),
             pltpu.VMEM((2, keys, queries), F32),
             pltpu.VMEM((2, keys, queries), F32),
-            pltpu.VMEM((2, keys, HEADS * queries), BF16),
-            pltpu.VMEM((2, keys, HEADS * queries), BF16),
+            pltpu.VMEM((2, HEADS * keys, queries), BF16),
+            pltpu.VMEM((2, HEADS * keys, queries), BF16),
+            pltpu.VMEM((HEADS * keys, features), F32),
+            pltpu.VMEM((HEADS * keys, features), F32),
         ],
         cost_estimate=pl.CostEstimate(
             flops=flops,
             bytes_accessed=3 * tokens.size * 2,
             transcendentals=blocks * queries * keys * HEADS,
         ),
-        compiler_params=pltpu.CompilerParams(vmem_limit_bytes=48 * 1024 * 1024),
+        compiler_params=pltpu.CompilerParams(vmem_limit_bytes=32 * 1024 * 1024),
     )(tokens, cot, pool_sums, w_query, w_key, w_value, w_out, gain, bias)
 
 
@@ -420,8 +479,9 @@
         normed_low = (standard * gain + bias_ref[...]).astype(BF16)
         key_grads = sums_ref[pl.ds(0, keys), :]
         value_grads = sums_ref[pl.ds(keys, keys), :]
-        d_key_ref[...] = split_dot(normed_low, key_grads) * grad_scale
-        d_value_ref[...] = split_dot(normed_low, value_grads) * grad_scale
+        both = split_dot(normed_low, jnp.concatenate([key_grads, value_grads], 1)) * grad_scale
+        d_key_ref[...] = both[:, :features]
+        d_value_ref[...] = both[:, features:]
         d_normed = dot_nt(key_grads.astype(BF16), w_key_ref[...]) + dot_nt(
             value_grads.astype(BF16), w_value_ref[...]
         )
@@ -478,19 +538,16 @@
         ],
         out_specs=(tile, square, square, square, square, line, line, whole(keys, features)),
         scratch_shapes=[pltpu.VMEM((keys, features), F32)],
-        compiler_params=pltpu.CompilerParams(vmem_limit_bytes=32 * 1024 * 1024),
+        compiler_params=pltpu.CompilerParams(vmem_limit_bytes=16 * 1024 * 1024),
     )(sums, pool_sums, dq, w_query, w_key, w_value, gain, bias)
 
 
 def body(tokens, cotangent, w_query, w_key, w_value, w_out, ln_gain, ln_bias):
     devices = lax.axis_size("gz")
     _, rows_y, plane_x, features = tokens.shape
-    cells_y, cells_x = rows_y // POOL, plane_x // POOL
+    cells_y = rows_y // POOL
     slab_rows = rows_y * plane_x
-    part = jnp.sum(
-        tokens.astype(F32).reshape(cells_y, POOL, cells_x, POOL, features), axis=(1, 3)
-    ).reshape(cells_y * cells_x, features)
-    pool_sums = exchange_pools(part)
+    pool_sums = exchange_pools(tokens.reshape(cells_y, POOL, plane_x, features))
     gain, bias = ln_gain.reshape(1, features), ln_bias.reshape(1, features)
     blocks = slab_rows // QUERIES
     sums, dq = attend(

time: 150 us -> 143 us (0.953)
  other arithmetic: 2.71 us -> 0 us
  local copies, waits for them, and re-layouts: 5.82 us -> 3.21 us
    pallas_call x1, Pallas kernels: 28.5 us -> 25.3 us  [sum_devices(): pl.pallas_call(sum_kernel, name='sum_devices', out_shape=jax.ShapeDtypeSt...]
    reduce_sum x1 -> x0, other arithmetic: 2.71 us -> none  [body(): jnp.sum(tokens.astype(F32).reshape(cells_y, POOL, cells_x, POOL, features...]
    unnamed x26 -> x18, local copies, waits for them, and re-layouts: 5.82 us -> 3.21 us
    pallas_call x1, Pallas kernels: 26 us -> 27.9 us  [exchange_pools(): pl.pallas_call(pool_kernel, name='pool_exchange', out_shape=jax.ShapeDtyp...]
where the time goes in v2:
time: 143 us
  Pallas kernels  139 us (97%)
  local copies, waits for them, and re-layouts  3.21 us (2%)
    pallas_call x1, Pallas kernels, attend(): pl.pallas_call(attend_kernel, name='attend', out_shape=(jax.ShapeDtypeStr...  80.6 us
    pallas_call x1, Pallas kernels, exchange_pools(): pl.pallas_call(pool_kernel, name='pool_exchange', out_shape=jax.ShapeDtyp...  27.9 us
    pallas_call x1, Pallas kernels, sum_devices(): pl.pallas_call(sum_kernel, name='sum_devices', out_shape=jax.ShapeDtypeSt...  25.3 us
    pallas_call x1, Pallas kernels, finish(): pl.pallas_call(functools.partial(finish_kernel, grad_scale), name='finish...  4.84 us
    unnamed x18, local copies, waits for them, and re-layouts  3.21 us

profile of v2, /device:TPU:1, one launch (start us, length us, event | category | flops | bytes accessed | tf_op | source)
XLA Modules:
  0.0 142.7 jit_solution(4457466246631858452)
XLA Ops:
  0.6 0.0 copy-start.6
  0.6 0.0 copy-start.5
  0.7 0.0 copy-start
  0.7 1.6 %copy-done = bf16[1,64,128,128]{3,2,1,0:T(8,128)(2,1)S(1)} copy-done((bf16[1,64,128,128]{3,2,1,0:T(8,128)(2,1)S(1)}, bf16[1,64,128,128]{3,2,1,0:T(8,128)(2,1)}, u32[]{:S(2)}) %copy-start) | copy-done | bytes 2097176
  2.3 0.0 copy-start.1
  2.3 0.0 copy-start.2
  2.3 0.0 copy-start.3
  2.3 0.0 copy-start.4
  2.3 0.0 copy-start.8
  2.3 27.9 %pool_exchange.1.pool_ref = f32[512,128]{1,0:T(8,128)S(1)} custom-call(bf16[4,16,128,128]{3,2,1,0:T(8,128)(2,1)S(1)} %bitcast.12), custom_call_target="tpu_custom_call" | custom-call | tf_op jit(solution)/shard_map/pool_exchange/pallas_call | solution.py:111
  30.2 0.0 copy-done.6
  30.2 0.0 copy-done.5
  30.3 0.0 copy-done.1
  30.3 0.0 copy-done.2
  30.3 0.0 copy-done.3
  30.3 0.0 copy-done.4
  30.3 0.0 copy-done.8
  30.3 0.0 copy-start.7
  30.3 1.6 %copy-done.7 = bf16[1,64,128,128]{3,2,1,0:T(8,128)(2,1)S(1)} copy-done((bf16[1,64,128,128]{3,2,1,0:T(8,128)(2,1)S(1)}, bf16[1,64,128,128]{3,2,1,0:T(8,128)(2,1)}, u32[]{:S(2)}) %copy-start.7) | copy-done | bytes 2097176
  31.9 80.6 %attend.1 = (f32[1280,128]{1,0:T(8,128)S(1)}, bf16[32,256,128]{2,1,0:T(8,128)(2,1)S(1)}) custom-call(bf16[32,256,128]{2,1,0:T(8,128)(2,1)S(1)} %bitcast.13, bf16[32,256,128]{2,1,0:T(8,128)(2,1)S(1)} %bitcast.20, f32[512,128]{1,0:T(8,128)S(1)} %pool_exchange.1.pool_ref, bf16[128,128]{1,0:T(8,128)(2,1)S(1)} %copy-done.2, bf16[128,128]{1,0:T(8,128)(2,1)S(1)} %copy-done.3, ...), custom_call_target="tpu_custom_call" | custom-call | flops 8053063680 | bytes 6291456 | tf_op jit(solution)/shard_map/attend/pallas_call | solution.py:422
  112.5 25.3 %sum_devices.1 = f32[32,40,128]{2,1,0:T(8,128)S(1)} custom-call(f32[32,40,128]{2,1,0:T(8,128)S(1)} %bitcast.15), custom_call_target="tpu_custom_call" | custom-call | tf_op jit(solution)/shard_map/sum_devices/pallas_call | solution.py:225
  137.8 4.8 %finish.1 = (bf16[8192,128]{1,0:T(8,128)(2,1)}, f32[128,128]{1,0:T(8,128)}, f32[128,128]{1,0:T(8,128)}, f32[128,128]{1,0:T(8,128)}, f32[128,128]{1,0:T(8,128)}, ...) custom-call(f32[1280,128]{1,0:T(8,128)S(1)} %bitcast.11, f32[512,128]{1,0:T(8,128)S(1)} %pool_exchange.1.pool_ref, ...), custom_call_target="tpu_custom_call" | custom-call | tf_op jit(solution)/shard_map/finish/pallas_call | solution.py:526
Async XLA Ops:
  0.6 29.6 %copy-start.6 = (f32[128]{0:T(128)S(1)}, f32[128]{0:T(128)}, u32[]{:S(2)}) copy-start(f32[128]{0:T(128)} %param.15) | copy-start | bytes 1540
  0.6 29.6 %copy-start.5 = (f32[128]{0:T(128)S(1)}, f32[128]{0:T(128)}, u32[]{:S(2)}) copy-start(f32[128]{0:T(128)} %param.14) | copy-start | bytes 1540
  0.7 1.6 %copy-start = (bf16[1,64,128,128]{3,2,1,0:T(8,128)(2,1)S(1)}, bf16[1,64,128,128]{3,2,1,0:T(8,128)(2,1)}, u32[]{:S(2)}) copy-start(bf16[1,64,128,128]{3,2,1,0:T(8,128)(2,1)} %param.8) | copy-start | bytes 6291460
  2.3 28.0 %copy-start.1 = (bf16[1,64,128,128]{3,2,1,0:T(8,128)(2,1)S(1)}, bf16[1,64,128,128]{3,2,1,0:T(8,128)(2,1)}, u32[]{:S(2)}) copy-start(bf16[1,64,128,128]{3,2,1,0:T(8,128)(2,1)} %param.8) | copy-start | bytes 6291460
  2.3 28.0 %copy-start.2 = (bf16[128,128]{1,0:T(8,128)(2,1)S(1)}, bf16[128,128]{1,0:T(8,128)(2,1)}, u32[]{:S(2)}) copy-start(bf16[128,128]{1,0:T(8,128)(2,1)} %w_query_ref.3) | copy-start | bytes 98308
  2.3 28.0 %copy-start.3 = (bf16[128,128]{1,0:T(8,128)(2,1)S(1)}, bf16[128,128]{1,0:T(8,128)(2,1)}, u32[]{:S(2)}) copy-start(bf16[128,128]{1,0:T(8,128)(2,1)} %w_key_ref.3) | copy-start | bytes 98308
  2.3 28.0 %copy-start.4 = (bf16[128,128]{1,0:T(8,128)(2,1)S(1)}, bf16[128,128]{1,0:T(8,128)(2,1)}, u32[]{:S(2)}) copy-start(bf16[128,128]{1,0:T(8,128)(2,1)} %w_value_ref.3) | copy-start | bytes 98308
  2.3 28.0 %copy-start.8 = (bf16[128,128]{1,0:T(8,128)(2,1)S(1)}, bf16[128,128]{1,0:T(8,128)(2,1)}, u32[]{:S(2)}) copy-start(bf16[128,128]{1,0:T(8,128)(2,1)} %w_out_ref.1) | copy-start | bytes 98308
  30.3 1.6 %copy-start.7 = (bf16[1,64,128,128]{3,2,1,0:T(8,128)(2,1)S(1)}, bf16[1,64,128,128]{3,2,1,0:T(8,128)(2,1)}, u32[]{:S(2)}) copy-start(bf16[1,64,128,128]{3,2,1,0:T(8,128)(2,1)} %param.9) | copy-start | bytes 6291460

commit v3 on v2

--- a/solution.py
+++ b/solution.py
@@ -17,7 +17,7 @@
 
 Z = 8
 PLANE = 16
-QUERIES = 256
+QUERIES = 512
 KEY_CHUNK = 128
 SAFE_LOG2 = 60.0
 
@@ -50,12 +50,30 @@
     return copy
 
 
+LOADS = 4
+
+
 def pool_kernel(
-    tokens_ref, out_ref, pieces, got, near, far, sum_send, sum_recv, near_send, near_recv,
-    far_send, far_recv,
+    tokens_hbm, cot_hbm, w_query_ref, w_out_ref, out_ref, tokens_ref, cot_ref, q_rows, q_cols,
+    d_rows, d_cols, norm_ref, pieces, got, near, far, load_sem, sum_send, sum_recv, near_send,
+    near_recv, far_send, far_recv,
 ):
-    cells_y, _, plane_x, features = tokens_ref.shape
+    blocks, queries, features = tokens_ref.shape
+    head_dim = features // HEADS
+    plane_x = queries // 4
     cells_x = plane_x // POOL
+    part = blocks // LOADS
+    loads = [
+        pltpu.make_async_copy(
+            source.at[pl.ds(n * part, part)], target.at[pl.ds(n * part, part)],
+            load_sem.at[k, n],
+        )
+        for k, (source, target) in enumerate(((tokens_hbm, tokens_ref), (cot_hbm, cot_ref)))
+        for n in range(LOADS)
+    ]
+    for load in loads:
+        load.start()
+
     me = lax.axis_index("gz")
     core, chip = lax.rem(me, 2), me // 2
     member, block = lax.rem(chip, 16), chip // 16
@@ -69,8 +87,13 @@
     await_partners = greet(near_ids + far_ids)
 
     share = got.shape[1]
-    for y in range(cells_y):
-        rows = jnp.sum(tokens_ref[y].astype(F32), axis=0)
+    for y in range(LOADS):
+        loads[y].wait()
+        rows = jnp.zeros((plane_x, features), F32)
+        for b in range(y * part, (y + 1) * part):
+            wide = tokens_ref[b].astype(F32)
+            for k in range(queries // plane_x):
+                rows = rows + wide[k * plane_x : (k + 1) * plane_x, :]
         cells = jnp.sum(rows.reshape(cells_x, POOL, features), axis=1)
         for x in range(cells_x // share):
             pieces[y * (cells_x // share) + x] = cells[x * share : (x + 1) * share, :]
@@ -79,16 +102,42 @@
         send(pieces.at[members[t]], got.at[t], sum_send.at[t], sum_recv.at[t], near_ids[t])
         for t in range(15)
     ]
+
+    w_query = w_query_ref[...]
+    w_query_t = transposed(w_query)
+    w_out = w_out_ref[...]
+    w_out_t = transposed(w_out)
+
+    def project_tokens(i, norm):
+        rows = tokens_ref[i]
+        q_rows[i] = dot(rows, w_query).astype(BF16)
+        cols = dot_nt(w_query_t, rows).astype(BF16)
+        q_cols[i] = cols
+        wide = cols.astype(F32).reshape(HEADS, head_dim, queries)
+        return jnp.maximum(norm, jnp.sum(wide * wide, axis=1))
+
+    def project_grads(i, carry):
+        grads = cot_ref[i]
+        d_rows[i] = dot(grads, w_out_t).astype(BF16)
+        d_cols[i] = dot_nt(w_out, grads).astype(BF16)
+        return carry
+
+    norm_ref[...] = lax.fori_loop(
+        0, blocks, project_tokens, jnp.zeros((HEADS, queries), F32)
+    )
+
     total = pieces[member]
     for t in range(15):
         copies[t].wait()
         total = total + got[t]
-
     near[member] = total
     copies = [
         send(near.at[member], near.at[member], near_send.at[t], near_recv.at[t], near_ids[t])
         for t in range(15)
     ]
+    for load in loads[LOADS:]:
+        load.wait()
+    lax.fori_loop(0, blocks // 2, project_grads, 0)
     for copy in copies:
         copy.wait()
     for m in range(16):
@@ -98,33 +147,43 @@
         send(far.at[group], far.at[group], far_send.at[t], far_recv.at[t], far_ids[t])
         for t in range(15)
     ]
+    lax.fori_loop(blocks // 2, blocks, project_grads, 0)
     for copy in copies:
         copy.wait()
     for g in range(16):
         out_ref[pl.ds(g * 32, 32), :] = far[g]
 
 
-def exchange_pools(tokens):
-    cells_y, _, plane_x, features = tokens.shape
-    rows = cells_y * (plane_x // POOL)
+def exchange_pools(tokens, cot, w_query, w_out):
+    blocks, queries, features = tokens.shape
+    rows = 32
     dma = pltpu.SemaphoreType.DMA
+    vmem = pl.BlockSpec(memory_space=pltpu.VMEM)
+    hbm = pl.BlockSpec(memory_space=pl.ANY)
+    by_rows = jax.ShapeDtypeStruct((blocks, queries, features), BF16)
+    by_cols = jax.ShapeDtypeStruct((blocks, features, queries), BF16)
     return pl.pallas_call(
         pool_kernel,
         name="pool_exchange",
-        out_shape=jax.ShapeDtypeStruct((16 * rows, features), F32),
-        in_specs=[pl.BlockSpec(memory_space=pltpu.VMEM)],
-        out_specs=pl.BlockSpec(memory_space=pltpu.VMEM),
+        out_shape=(
+            jax.ShapeDtypeStruct((16 * rows, features), F32),
+            by_rows, by_rows, by_rows, by_cols, by_rows, by_cols,
+            jax.ShapeDtypeStruct((HEADS, queries), F32),
+        ),
+        in_specs=[hbm, hbm, vmem, vmem],
+        out_specs=(vmem,) * 8,
         scratch_shapes=[
             pltpu.VMEM((16, rows // 16, features), F32),
             pltpu.VMEM((15, rows // 16, features), F32),
             pltpu.VMEM((16, rows // 16, features), F32),
             pltpu.VMEM((16, rows, features), F32),
+            dma((2, LOADS)),
             *[dma((15,))] * 6,
         ],
         compiler_params=pltpu.CompilerParams(
-            collective_id=0, has_side_effects=True, vmem_limit_bytes=8 * 1024 * 1024
+            collective_id=0, has_side_effects=True, vmem_limit_bytes=40 * 1024 * 1024
         ),
-    )(tokens)
+    )(tokens, cot, w_query, w_out)
 
 
 STREAMS = ((0, 24), (24, 16))
@@ -279,8 +338,8 @@
 
 
 def attend_kernel(
-    tokens_ref, cot_ref, pool_ref, w_query_ref, w_key_ref, w_value_ref, w_out_ref, gain_ref,
-    bias_ref, sums_ref, dq_ref, q_rows, q_cols, d_rows, d_cols, key_terms, value_terms, key_cols,
+    tokens_ref, cot_ref, pool_ref, q_rows, q_cols, d_rows, d_cols, norm_ref, w_key_ref,
+    w_value_ref, gain_ref, bias_ref, sums_ref, dq_ref, key_terms, value_terms, key_cols,
     value_cols, exps, dps, probs, dscores, key_sums, value_sums,
 ):
     blocks, queries, features = tokens_ref.shape
@@ -311,23 +370,7 @@
     key_wide = key_cols[...].astype(F32).reshape(HEADS, head_dim, keys)
     key_norm = jnp.max(jnp.sum(key_wide * key_wide, axis=1), axis=1, keepdims=True)
 
-    w_query = w_query_ref[...]
-    w_query_t = transposed(w_query)
-    w_out = w_out_ref[...]
-    w_out_t = transposed(w_out)
-
-    def project(i, norm):
-        rows, grads = tokens_ref[i], cot_ref[i]
-        q_rows[i] = dot(rows, w_query).astype(BF16)
-        d_rows[i] = dot(grads, w_out_t).astype(BF16)
-        cols = dot_nt(w_query_t, rows).astype(BF16)
-        q_cols[i] = cols
-        d_cols[i] = dot_nt(w_out, grads).astype(BF16)
-        wide = cols.astype(F32).reshape(HEADS, head_dim, queries)
-        return jnp.maximum(norm, jnp.sum(wide * wide, axis=1))
-
-    norm = lax.fori_loop(0, blocks, project, jnp.zeros((HEADS, queries), F32))
-    bound = jnp.max(norm * key_norm) * (scale * math.log2(math.e)) ** 2
+    bound = jnp.max(norm_ref[...] * key_norm) * (scale * math.log2(math.e)) ** 2
 
     sums_ref[...] = jnp.zeros_like(sums_ref)
     key_sums[...] = jnp.zeros_like(key_sums)
@@ -356,7 +399,7 @@
             delta = delta + fold(e * dp)
         return total, delta
 
-    def second(h, slot, bank, sums):
+    def second(h, slot, sums):
         total, delta = (jnp.sum(x, axis=0, keepdims=True) for x in sums)
         inverse = 1.0 / total
         delta = delta * inverse
@@ -364,48 +407,51 @@
             part = pl.ds(c * KEY_CHUNK, KEY_CHUNK)
             rows = pl.ds(h * keys + c * KEY_CHUNK, KEY_CHUNK)
             p = exps[slot, part, :] * inverse
-            probs[bank, rows, :] = p.astype(BF16)
-            dscores[bank, rows, :] = (p * (dps[slot, part, :] - delta)).astype(BF16)
+            probs[rows, :] = p.astype(BF16)
+            dscores[rows, :] = (p * (dps[slot, part, :] - delta)).astype(BF16)
         head = pl.ds(h * head_dim, head_dim)
         rows = pl.ds(h * keys, keys)
-        attn = dot(value_cols[head, :], probs[bank, rows, :])
-        dq = dot(key_cols[head, :], dscores[bank, rows, :])
+        attn = dot(value_cols[head, :], probs[rows, :])
+        dq = dot(key_cols[head, :], dscores[rows, :])
         return attn, dq
 
-    def third(i, bank, outs):
+    def over_keys(i, outs):
         attn_low = jnp.concatenate([o[0] for o in outs], axis=0).astype(BF16)
         dq_low = jnp.concatenate([o[1] for o in outs], axis=0).astype(BF16)
         sums_ref[pl.ds(2 * keys, features), :] += dot(dq_low, tokens_ref[i])
         sums_ref[pl.ds(2 * keys + features, features), :] += dot(attn_low, cot_ref[i])
         dq_ref[i] = dq_low.astype(F32).T.astype(BF16)
-        key_sums[...] += dot(dscores[bank], q_rows[i])
-        value_sums[...] += dot(probs[bank], d_rows[i])
-
-    def run(at_once, safe):
-        def step(j, carry):
-            units = [(b, h) for b in range(at_once) for h in range(HEADS)]
-            pending = first(j * at_once, 0, 0, safe)
+
+    def over_queries(i):
+        key_sums[...] += dot(dscores[...], q_rows[i])
+        value_sums[...] += dot(probs[...], d_rows[i])
+
+    def run(safe):
+        def step(i, carry):
+            pending = [first(i, 0, 0, safe), first(i, 1, 1, safe)]
+            over_queries(jnp.maximum(i - 1, 0))
             outs = []
-            for n, (b, h) in enumerate(units):
-                current = pending
-                if n + 1 < len(units):
-                    nb, nh = units[n + 1]
-                    pending = first(j * at_once + nb, nh, (n + 1) % 2, safe)
-                outs.append(second(h, n % 2, b, current))
-                if h == HEADS - 1:
-                    third(j * at_once + b, b, outs)
-                    outs = []
+            for h in range(HEADS):
+                outs.append(second(h, h % 2, pending[h]))
+                if h + 2 < HEADS:
+                    pending.append(first(i, h + 2, h % 2, safe))
+            over_keys(i, outs)
             return carry
 
-        lax.fori_loop(0, blocks // at_once, step, 0)
+        lax.fori_loop(0, blocks, step, 0)
+
+    probs[...] = jnp.zeros_like(probs)
+    dscores[...] = jnp.zeros_like(dscores)
 
     @pl.when(bound <= SAFE_LOG2**2)
     def _():
-        run(2, False)
+        run(False)
 
     @pl.when(jnp.logical_not(bound <= SAFE_LOG2**2))
     def _():
-        run(1, True)
+        run(True)
+
+    over_queries(blocks - 1)
 
     for start, wide in ((0, key_sums), (keys, value_sums)):
         total = wide[pl.ds(0, keys), :]
@@ -414,10 +460,10 @@
         sums_ref[pl.ds(start, keys), :] = total
 
 
-def attend(tokens, cot, pool_sums, w_query, w_key, w_value, w_out, gain, bias):
+def attend(tokens, cot, pool_sums, q_rows, q_cols, d_rows, d_cols, norm, w_key, w_value, gain, bias):
     blocks, queries, features = tokens.shape
     keys = pool_sums.shape[0]
-    flops = 2 * blocks * queries * features * (6 * keys + 6 * features)
+    flops = 2 * blocks * queries * features * (6 * keys + 2 * features)
     vmem = pl.BlockSpec(memory_space=pltpu.VMEM)
     return pl.pallas_call(
         attend_kernel,
@@ -426,21 +472,17 @@
             jax.ShapeDtypeStruct((2 * keys + 2 * features, features), F32),
             jax.ShapeDtypeStruct((blocks, queries, features), BF16),
         ),
-        in_specs=[vmem] * 9,
+        in_specs=[vmem] * 12,
         out_specs=(vmem, vmem),
         scratch_shapes=[
-            pltpu.VMEM((blocks, queries, features), BF16),
-            pltpu.VMEM((blocks, features, queries), BF16),
-            pltpu.VMEM((blocks, queries, features), BF16),
-            pltpu.VMEM((blocks, features, queries), BF16),
             pltpu.VMEM((HEADS, keys, features), BF16),
             pltpu.VMEM((HEADS, keys, features), BF16),
             pltpu.VMEM((features, keys), BF16),
             pltpu.VMEM((features, keys), BF16),
             pltpu.VMEM((2, keys, queries), F32),
             pltpu.VMEM((2, keys, queries), F32),
-            pltpu.VMEM((2, HEADS * keys, queries), BF16),
-            pltpu.VMEM((2, HEADS * keys, queries), BF16),
+            pltpu.VMEM((HEADS * keys, queries), BF16),
+            pltpu.VMEM((HEADS * keys, queries), BF16),
             pltpu.VMEM((HEADS * keys, features), F32),
             pltpu.VMEM((HEADS * keys, features), F32),
         ],
@@ -449,8 +491,8 @@
             bytes_accessed=3 * tokens.size * 2,
             transcendentals=blocks * queries * keys * HEADS,
         ),
-        compiler_params=pltpu.CompilerParams(vmem_limit_bytes=32 * 1024 * 1024),
-    )(tokens, cot, pool_sums, w_query, w_key, w_value, w_out, gain, bias)
+        compiler_params=pltpu.CompilerParams(vmem_limit_bytes=28 * 1024 * 1024),
+    )(tokens, cot, pool_sums, q_rows, q_cols, d_rows, d_cols, norm, w_key, w_value, gain, bias)
 
 
 def split_dot(low, wide):
@@ -515,7 +557,7 @@
 def finish(sums, pool_sums, dq, w_query, w_key, w_value, gain, bias, grad_scale):
     keys, features = pool_sums.shape
     tokens = dq.shape[0]
-    rows = 1024
+    rows = 2048
 
     def whole(*shape):
         return pl.BlockSpec(shape, lambda i: (0,) * len(shape))
@@ -545,15 +587,17 @@
 def body(tokens, cotangent, w_query, w_key, w_value, w_out, ln_gain, ln_bias):
     devices = lax.axis_size("gz")
     _, rows_y, plane_x, features = tokens.shape
-    cells_y = rows_y // POOL
     slab_rows = rows_y * plane_x
-    pool_sums = exchange_pools(tokens.reshape(cells_y, POOL, plane_x, features))
     gain, bias = ln_gain.reshape(1, features), ln_bias.reshape(1, features)
     blocks = slab_rows // QUERIES
-    sums, dq = attend(
+    pool_sums, token_rows, cot_rows, q_rows, q_cols, d_rows, d_cols, norm = exchange_pools(
         tokens.reshape(blocks, QUERIES, features),
         cotangent.reshape(blocks, QUERIES, features),
-        pool_sums, w_query, w_key, w_value, w_out, gain, bias,
+        w_query, w_out,
+    )
+    sums, dq = attend(
+        token_rows, cot_rows, pool_sums, q_rows, q_cols, d_rows, d_cols, norm, w_key, w_value,
+        gain, bias,
     )
     sums = sum_devices(sums)
     grad_scale = float(devices * slab_rows) ** (-0.5)

time: 143 us -> 135 us (0.944)
  Pallas kernels: 139 us -> 133 us
  local copies, waits for them, and re-layouts: 3.21 us -> 1.53 us
    pallas_call x1, Pallas kernels: 80.6 us -> 76.2 us  [attend(): pl.pallas_call(attend_kernel, name='attend', out_shape=(jax.ShapeDtypeStr...]
    unnamed x18 -> x14, local copies, waits for them, and re-layouts: 3.21 us -> 1.53 us
    pallas_call x1, Pallas kernels: 4.84 us -> 3.38 us  [finish(): pl.pallas_call(functools.partial(finish_kernel, grad_scale), name='finish...]
where the time goes in v3:
time: 135 us
  Pallas kernels  133 us (99%)
  local copies, waits for them, and re-layouts  1.53 us (1%)
    pallas_call x1, Pallas kernels, attend(): pl.pallas_call(attend_kernel, name='attend', out_shape=(jax.ShapeDtypeStr...  76.2 us
    pallas_call x1, Pallas kernels, exchange_pools(): pl.pallas_call(pool_kernel, name='pool_exchange', out_shape=(jax.ShapeDty...  28 us
    pallas_call x1, Pallas kernels, sum_devices(): pl.pallas_call(sum_kernel, name='sum_devices', out_shape=jax.ShapeDtypeSt...  25.3 us
    pallas_call x1, Pallas kernels, finish(): pl.pallas_call(functools.partial(finish_kernel, grad_scale), name='finish...  3.38 us

profile of v3, /device:TPU:1, one launch (start us, length us, event | category | flops | bytes accessed | tf_op | source)
XLA Modules:
  0.0 135.1 jit_solution(13601831215292770582)
XLA Ops:
  0.6 0.0 copy-start
  0.6 0.7 copy-done
  1.4 0.0 copy-start.2
  1.4 0.8 copy-done.2
  2.2 0.0 copy-start.3
  2.2 0.0 copy-start.4
  2.2 0.0 copy-start.5
  2.2 0.0 copy-start.6
  2.2 28.0 %pool_exchange.1 = (f32[512,128]{1,0:T(8,128)S(1)}, bf16[16,512,128]{2,1,0:T(8,128)(2,1)S(1)}, bf16[16,512,128]{2,1,0:T(8,128)(2,1)S(1)}, bf16[16,512,128]{2,1,0...) custom-call(bf16[16,512,128]{2,1,0:T(8,128)(2,1)} %bitcast.17, ...), custom_call_target="tpu_custom_call" | custom-call | tf_op jit(solution)/shard_map/pool_exchange/pallas_call | solution.py:165
  30.2 0.0 copy-done.3
  30.2 0.0 copy-done.4
  30.2 0.0 copy-done.5
  30.2 0.0 copy-done.6
  30.2 0.0 copy-start.1
  30.3 76.2 %attend.1 = (f32[1280,128]{1,0:T(8,128)S(1)}, bf16[16,512,128]{2,1,0:T(8,128)(2,1)S(1)}) custom-call(bf16[16,512,128]{2,1,0:T(8,128)(2,1)S(1)} %get-tuple-element.26.tokens_ref, bf16[16,512,128]{2,1,0:T(8,128)(2,1)S(1)} %get-tuple-element.27.cot_ref, f32[512,128]{1,0:T(8,128)S(1)} %get-tuple-element.28.pool_ref, ...), custom_call_target="tpu_custom_call" | custom-call | flops 6979321856 | bytes 6291456 | tf_op jit(solution)/shard_map/attend/pallas_call | solution.py:468
  106.4 25.3 %sum_devices.1 = f32[32,40,128]{2,1,0:T(8,128)S(1)} custom-call(f32[32,40,128]{2,1,0:T(8,128)S(1)} %bitcast.12), custom_call_target="tpu_custom_call" | custom-call | tf_op jit(solution)/shard_map/sum_devices/pallas_call | solution.py:284
  131.7 0.0 copy-done.1
  131.7 3.4 %finish.1 = (bf16[8192,128]{1,0:T(8,128)(2,1)}, f32[128,128]{1,0:T(8,128)}, f32[128,128]{1,0:T(8,128)}, f32[128,128]{1,0:T(8,128)}, f32[128,128]{1,0:T(8,128)}, ...) custom-call(f32[1280,128]{1,0:T(8,128)S(1)} %bitcast.10, f32[512,128]{1,0:T(8,128)S(1)} %get-tuple-element.28.pool_ref, ...), custom_call_target="tpu_custom_call" | custom-call | tf_op jit(solution)/shard_map/finish/pallas_call | solution.py:568
Async XLA Ops:
  0.6 0.8 copy-start
  1.4 0.8 copy-start.2
  2.2 28.1 %copy-start.3 = (bf16[128,128]{1,0:T(8,128)(2,1)S(1)}, bf16[128,128]{1,0:T(8,128)(2,1)}, u32[]{:S(2)}) copy-start(bf16[128,128]{1,0:T(8,128)(2,1)} %w_key_ref.3) | copy-start | bytes 98308
  2.2 28.1 %copy-start.4 = (bf16[128,128]{1,0:T(8,128)(2,1)S(1)}, bf16[128,128]{1,0:T(8,128)(2,1)}, u32[]{:S(2)}) copy-start(bf16[128,128]{1,0:T(8,128)(2,1)} %w_value_ref.3) | copy-start | bytes 98308
  2.2 28.1 %copy-start.5 = (f32[128]{0:T(128)S(1)}, f32[128]{0:T(128)}, u32[]{:S(2)}) copy-start(f32[128]{0:T(128)} %param.14) | copy-start | bytes 1540
  2.2 28.1 %copy-start.6 = (f32[128]{0:T(128)S(1)}, f32[128]{0:T(128)}, u32[]{:S(2)}) copy-start(f32[128]{0:T(128)} %param.15) | copy-start | bytes 1540
  30.2 101.5 %copy-start.1 = (bf16[128,128]{1,0:T(8,128)(2,1)S(1)}, bf16[128,128]{1,0:T(8,128)(2,1)}, u32[]{:S(2)}) copy-start(bf16[128,128]{1,0:T(8,128)(2,1)} %w_query_ref.3) | copy-start | bytes 98308

commit v4 on v3

--- a/solution.py
+++ b/solution.py
@@ -1,5 +1,4 @@
 import functools
-import math
 
 import jax
 import jax.numpy as jnp
@@ -18,8 +17,8 @@
 Z = 8
 PLANE = 16
 QUERIES = 512
-KEY_CHUNK = 128
-SAFE_LOG2 = 60.0
+KEY_CHUNK = 256
+SAFE = 40.0
 
 
 def dot(a, b):
@@ -54,7 +53,7 @@
 
 
 def pool_kernel(
-    tokens_hbm, cot_hbm, w_query_ref, w_out_ref, out_ref, tokens_ref, cot_ref, q_rows, q_cols,
+    tokens_hbm, cot_hbm, weights_ref, out_ref, tokens_ref, cot_ref, q_rows, q_cols,
     d_rows, d_cols, norm_ref, pieces, got, near, far, load_sem, sum_send, sum_recv, near_send,
     near_recv, far_send, far_recv,
 ):
@@ -103,9 +102,9 @@
         for t in range(15)
     ]
 
-    w_query = w_query_ref[...]
+    w_query = weights_ref[:features, :]
     w_query_t = transposed(w_query)
-    w_out = w_out_ref[...]
+    w_out = weights_ref[features:, :]
     w_out_t = transposed(w_out)
 
     def project_tokens(i, norm):
@@ -154,7 +153,7 @@
         out_ref[pl.ds(g * 32, 32), :] = far[g]
 
 
-def exchange_pools(tokens, cot, w_query, w_out):
+def exchange_pools(tokens, cot, weights):
     blocks, queries, features = tokens.shape
     rows = 32
     dma = pltpu.SemaphoreType.DMA
@@ -170,7 +169,7 @@
             by_rows, by_rows, by_rows, by_cols, by_rows, by_cols,
             jax.ShapeDtypeStruct((HEADS, queries), F32),
         ),
-        in_specs=[hbm, hbm, vmem, vmem],
+        in_specs=[hbm, hbm, vmem],
         out_specs=(vmem,) * 8,
         scratch_shapes=[
             pltpu.VMEM((16, rows // 16, features), F32),
@@ -183,7 +182,7 @@
         compiler_params=pltpu.CompilerParams(
             collective_id=0, has_side_effects=True, vmem_limit_bytes=40 * 1024 * 1024
         ),
-    )(tokens, cot, w_query, w_out)
+    )(tokens, cot, weights)
 
 
 STREAMS = ((0, 24), (24, 16))
@@ -340,7 +339,7 @@
 def attend_kernel(
     tokens_ref, cot_ref, pool_ref, q_rows, q_cols, d_rows, d_cols, norm_ref, w_key_ref,
     w_value_ref, gain_ref, bias_ref, sums_ref, dq_ref, key_terms, value_terms, key_cols,
-    value_cols, exps, dps, probs, dscores, key_sums, value_sums,
+    value_cols, exps, dps, probs, dscores, key_sums, value_sums, attn_low, dq_low,
 ):
     blocks, queries, features = tokens_ref.shape
     keys = pool_ref.shape[0]
@@ -358,7 +357,7 @@
     lane = lax.broadcasted_iota(jnp.int32, (keys, features), 1)
     lane_group = lane // head_dim
     for w_ref, factor, terms, cols in (
-        (w_key_ref, scale * math.log2(math.e), key_terms, key_cols),
+        (w_key_ref, scale, key_terms, key_cols),
         (w_value_ref, scale, value_terms, value_cols),
     ):
         w = w_ref[...]
@@ -370,7 +369,7 @@
     key_wide = key_cols[...].astype(F32).reshape(HEADS, head_dim, keys)
     key_norm = jnp.max(jnp.sum(key_wide * key_wide, axis=1), axis=1, keepdims=True)
 
-    bound = jnp.max(norm_ref[...] * key_norm) * (scale * math.log2(math.e)) ** 2
+    bound = jnp.max(norm_ref[...] * key_norm) * scale**2
 
     sums_ref[...] = jnp.zeros_like(sums_ref)
     key_sums[...] = jnp.zeros_like(key_sums)
@@ -378,80 +377,94 @@
     def fold(x):
         return jnp.sum(x.reshape(x.shape[0] // 8, 8, queries), axis=0)
 
-    def first(i, h, slot, safe):
-        query = q_cols[i, h * head_dim : (h + 1) * head_dim, :]
-        grad = d_cols[i, h * head_dim : (h + 1) * head_dim, :]
-        query = jnp.concatenate([query] * HEADS, axis=0)
-        grad = jnp.concatenate([grad] * HEADS, axis=0)
-        total = jnp.zeros((8, queries), F32)
-        delta = jnp.zeros((8, queries), F32)
-        scores = dot(key_terms[h], query)
-        d_probs = dot(value_terms[h], grad)
+    def operands(i, h):
+        head = pl.ds(h * head_dim, head_dim)
+        query, grad = q_cols[i, head, :], d_cols[i, head, :]
+        return jnp.concatenate([query] * HEADS, axis=0), jnp.concatenate([grad] * HEADS, axis=0)
+
+    def head_over_keys(h):
+        head = pl.ds(h * head_dim, head_dim)
+        rows = pl.ds(h * keys, keys)
+        attn_low[head, :] = dot(value_cols[head, :], probs[rows, :]).astype(BF16)
+        dq_low[head, :] = dot(key_cols[head, :], dscores[rows, :]).astype(BF16)
+
+    def block_over_keys(i):
+        dq = dq_low[...]
+        sums_ref[pl.ds(2 * keys, features), :] += dot(dq, tokens_ref[i])
+        sums_ref[pl.ds(2 * keys + features, features), :] += dot(attn_low[...], cot_ref[i])
+        dq_ref[i] = dq.astype(F32).T.astype(BF16)
+
+    def keys_over_queries(i, h):
+        rows = pl.ds(h * keys, keys)
+        key_sums[rows, :] += dot(dscores[rows, :], q_rows[i])
+
+    def values_over_queries(i, h):
+        rows = pl.ds(h * keys, keys)
+        value_sums[rows, :] += dot(probs[rows, :], d_rows[i])
+
+    def stage(i, h, sums, safe, only_first=False):
+        following = (h + 1) % HEADS
+        at = i if following else jnp.minimum(i + 1, blocks - 1)
+        summed = jnp.maximum(i - 1, 0) if following else i
+        query, grad = operands(at, following)
+        slot, later = h % 2, following % 2
+        if not only_first:
+            total, delta = (jnp.sum(x, axis=0, keepdims=True) for x in sums)
+            inverse = 1.0 / total
+            delta = delta * inverse
+        next_total = jnp.zeros((8, queries), F32)
+        next_delta = jnp.zeros((8, queries), F32)
         if safe:
+            scores = dot(key_terms[following], query)
             scores = scores - jnp.max(scores, axis=0, keepdims=True)
         for c in range(chunks):
             part = slice(c * KEY_CHUNK, (c + 1) * KEY_CHUNK)
-            e = jnp.exp2(scores[part, :])
-            dp = d_probs[part, :]
-            exps[slot, part, :] = e
-            dps[slot, part, :] = dp
-            total = total + fold(e)
-            delta = delta + fold(e * dp)
-        return total, delta
-
-    def second(h, slot, sums):
-        total, delta = (jnp.sum(x, axis=0, keepdims=True) for x in sums)
-        inverse = 1.0 / total
-        delta = delta * inverse
-        for c in range(chunks):
-            part = pl.ds(c * KEY_CHUNK, KEY_CHUNK)
-            rows = pl.ds(h * keys + c * KEY_CHUNK, KEY_CHUNK)
-            p = exps[slot, part, :] * inverse
-            probs[rows, :] = p.astype(BF16)
-            dscores[rows, :] = (p * (dps[slot, part, :] - delta)).astype(BF16)
-        head = pl.ds(h * head_dim, head_dim)
-        rows = pl.ds(h * keys, keys)
-        attn = dot(value_cols[head, :], probs[rows, :])
-        dq = dot(key_cols[head, :], dscores[rows, :])
-        return attn, dq
-
-    def over_keys(i, outs):
-        attn_low = jnp.concatenate([o[0] for o in outs], axis=0).astype(BF16)
-        dq_low = jnp.concatenate([o[1] for o in outs], axis=0).astype(BF16)
-        sums_ref[pl.ds(2 * keys, features), :] += dot(dq_low, tokens_ref[i])
-        sums_ref[pl.ds(2 * keys + features, features), :] += dot(attn_low, cot_ref[i])
-        dq_ref[i] = dq_low.astype(F32).T.astype(BF16)
-
-    def over_queries(i):
-        key_sums[...] += dot(dscores[...], q_rows[i])
-        value_sums[...] += dot(probs[...], d_rows[i])
+            s = scores[part, :] if safe else dot(key_terms[following, part, :], query)
+            dp = dot(value_terms[following, part, :], grad)
+            if not only_first:
+                if c == 0:
+                    head_over_keys((h - 1) % HEADS)
+                    keys_over_queries(summed, following)
+                if c == chunks - 1:
+                    values_over_queries(summed, following)
+                    if h == 0:
+                        block_over_keys(summed)
+                rows = pl.ds(h * keys + c * KEY_CHUNK, KEY_CHUNK)
+                p = exps[slot, part, :] * inverse
+                probs[rows, :] = p.astype(BF16)
+                dscores[rows, :] = (p * (dps[slot, part, :] - delta)).astype(BF16)
+            e = jnp.exp(s)
+            exps[later, part, :] = e
+            dps[later, part, :] = dp
+            next_total = next_total + fold(e)
+            next_delta = next_delta + fold(e * dp)
+        return next_total, next_delta
 
     def run(safe):
-        def step(i, carry):
-            pending = [first(i, 0, 0, safe), first(i, 1, 1, safe)]
-            over_queries(jnp.maximum(i - 1, 0))
-            outs = []
+        def step(i, sums):
             for h in range(HEADS):
-                outs.append(second(h, h % 2, pending[h]))
-                if h + 2 < HEADS:
-                    pending.append(first(i, h + 2, h % 2, safe))
-            over_keys(i, outs)
-            return carry
-
-        lax.fori_loop(0, blocks, step, 0)
-
-    probs[...] = jnp.zeros_like(probs)
-    dscores[...] = jnp.zeros_like(dscores)
-
-    @pl.when(bound <= SAFE_LOG2**2)
+                sums = stage(i, h, sums, safe)
+            return sums
+
+        sums = stage(jnp.int32(-1), HEADS - 1, None, safe, only_first=True)
+        lax.fori_loop(0, blocks, step, sums)
+
+    for ref in (probs, dscores, attn_low, dq_low):
+        ref[...] = jnp.zeros_like(ref)
+
+    @pl.when(bound <= SAFE**2)
     def _():
         run(False)
 
-    @pl.when(jnp.logical_not(bound <= SAFE_LOG2**2))
+    @pl.when(jnp.logical_not(bound <= SAFE**2))
     def _():
         run(True)
 
-    over_queries(blocks - 1)
+    head_over_keys(HEADS - 1)
+    block_over_keys(blocks - 1)
+    for h in range(1, HEADS):
+        keys_over_queries(blocks - 1, h)
+        values_over_queries(blocks - 1, h)
 
     for start, wide in ((0, key_sums), (keys, value_sums)):
         total = wide[pl.ds(0, keys), :]
@@ -485,6 +498,8 @@
             pltpu.VMEM((HEADS * keys, queries), BF16),
             pltpu.VMEM((HEADS * keys, features), F32),
             pltpu.VMEM((HEADS * keys, features), F32),
+            pltpu.VMEM((features, queries), BF16),
+            pltpu.VMEM((features, queries), BF16),
         ],
         cost_estimate=pl.CostEstimate(
             flops=flops,
@@ -593,7 +608,7 @@
     pool_sums, token_rows, cot_rows, q_rows, q_cols, d_rows, d_cols, norm = exchange_pools(
         tokens.reshape(blocks, QUERIES, features),
         cotangent.reshape(blocks, QUERIES, features),
-        w_query, w_out,
+        jnp.concatenate([w_query, w_out], axis=0),
     )
     sums, dq = attend(
         token_rows, cot_rows, pool_sums, q_rows, q_cols, d_rows, d_cols, norm, w_key, w_value,

time: 135 us -> 132 us (0.978)
  Pallas kernels: 133 us -> 130 us
  local copies, waits for them, and re-layouts: 1.53 us -> 0.03 us
    pallas_call x1, Pallas kernels: 76.2 us -> 73.7 us  [attend(): pl.pallas_call(attend_kernel, name='attend', out_shape=(jax.ShapeDtypeStr...]
    unnamed x14 -> x10, local copies, waits for them, and re-layouts: 1.53 us -> 0.03 us
where the time goes in v4:
time: 132 us
  Pallas kernels  130 us (98%)
    pallas_call x1, Pallas kernels, attend(): pl.pallas_call(attend_kernel, name='attend', out_shape=(jax.ShapeDtypeStr...  73.7 us
    pallas_call x1, Pallas kernels, exchange_pools(): pl.pallas_call(pool_kernel, name='pool_exchange', out_shape=(jax.ShapeDty...  28 us
    pallas_call x1, Pallas kernels, sum_devices(): pl.pallas_call(sum_kernel, name='sum_devices', out_shape=jax.ShapeDtypeSt...  25.3 us
    pallas_call x1, Pallas kernels, finish(): pl.pallas_call(functools.partial(finish_kernel, grad_scale), name='finish...  3.38 us

profile of v4, /device:TPU:1, one launch (start us, length us, event | category | flops | bytes accessed | tf_op | source)
XLA Modules:
  0.0 131.9 jit_solution(5802072380715110758)
XLA Ops:
  0.6 0.8 pad_maximum_fusion.weights_ref
  1.4 0.0 copy-start.1
  1.4 0.0 copy-start.2
  1.4 0.0 copy-start.3
  1.4 0.0 copy-start.4
  1.4 28.0 %pool_exchange.1 = (f32[512,128]{1,0:T(8,128)S(1)}, bf16[16,512,128]{2,1,0:T(8,128)(2,1)S(1)}, bf16[16,512,128]{2,1,0:T(8,128)(2,1)S(1)}, bf16[16,512,128]{2,1,0...) custom-call(bf16[16,512,128]{2,1,0:T(8,128)(2,1)} %bitcast.17, ...), custom_call_target="tpu_custom_call" | custom-call | tf_op jit(solution)/shard_map/pool_exchange/pallas_call | solution.py:164
  29.5 0.0 copy-done.1
  29.5 0.0 copy-done.2
  29.5 0.0 copy-done.3
  29.5 0.0 copy-done.4
  29.5 0.0 copy-start
  29.5 73.7 %attend.1 = (f32[1280,128]{1,0:T(8,128)S(1)}, bf16[16,512,128]{2,1,0:T(8,128)(2,1)S(1)}) custom-call(bf16[16,512,128]{2,1,0:T(8,128)(2,1)S(1)} %get-tuple-element.26.tokens_ref, bf16[16,512,128]{2,1,0:T(8,128)(2,1)S(1)} %get-tuple-element.27.cot_ref, f32[512,128]{1,0:T(8,128)S(1)} %get-tuple-element.28.pool_ref, ...), custom_call_target="tpu_custom_call" | custom-call | flops 6979321856 | bytes 6291456 | tf_op jit(solution)/shard_map/attend/pallas_call | solution.py:481
  103.2 25.3 %sum_devices.1 = f32[32,40,128]{2,1,0:T(8,128)S(1)} custom-call(f32[32,40,128]{2,1,0:T(8,128)S(1)} %bitcast.12), custom_call_target="tpu_custom_call" | custom-call | tf_op jit(solution)/shard_map/sum_devices/pallas_call | solution.py:283
  128.5 0.0 copy-done
  128.5 3.4 %finish.1 = (bf16[8192,128]{1,0:T(8,128)(2,1)}, f32[128,128]{1,0:T(8,128)}, f32[128,128]{1,0:T(8,128)}, f32[128,128]{1,0:T(8,128)}, f32[128,128]{1,0:T(8,128)}, ...) custom-call(f32[1280,128]{1,0:T(8,128)S(1)} %bitcast.10, f32[512,128]{1,0:T(8,128)S(1)} %get-tuple-element.28.pool_ref, ...), custom_call_target="tpu_custom_call" | custom-call | tf_op jit(solution)/shard_map/finish/pallas_call | solution.py:583
Async XLA Ops:
  1.4 28.1 %copy-start.1 = (bf16[128,128]{1,0:T(8,128)(2,1)S(1)}, bf16[128,128]{1,0:T(8,128)(2,1)}, u32[]{:S(2)}) copy-start(bf16[128,128]{1,0:T(8,128)(2,1)} %w_key_ref.3) | copy-start | bytes 98308
  1.4 28.1 %copy-start.2 = (bf16[128,128]{1,0:T(8,128)(2,1)S(1)}, bf16[128,128]{1,0:T(8,128)(2,1)}, u32[]{:S(2)}) copy-start(bf16[128,128]{1,0:T(8,128)(2,1)} %w_value_ref.3) | copy-start | bytes 98308
  1.4 28.1 %copy-start.3 = (f32[128]{0:T(128)S(1)}, f32[128]{0:T(128)}, u32[]{:S(2)}) copy-start(f32[128]{0:T(128)} %param.14) | copy-start | bytes 1540
  1.4 28.1 %copy-start.4 = (f32[128]{0:T(128)S(1)}, f32[128]{0:T(128)}, u32[]{:S(2)}) copy-start(f32[128]{0:T(128)} %param.15) | copy-start | bytes 1540
  29.5 99.0 %copy-start = (bf16[128,128]{1,0:T(8,128)(2,1)S(1)}, bf16[128,128]{1,0:T(8,128)(2,1)}, u32[]{:S(2)}) copy-start(bf16[128,128]{1,0:T(8,128)(2,1)} %w_query_ref.1) | copy-start | bytes 98308

commit v5 on v4

--- a/solution.py
+++ b/solution.py
@@ -53,8 +53,7 @@
 
 
 def pool_kernel(
-    tokens_hbm, cot_hbm, weights_ref, out_ref, tokens_ref, cot_ref, q_rows, q_cols,
-    d_rows, d_cols, norm_ref, pieces, got, near, far, load_sem, sum_send, sum_recv, near_send,
+    tokens_hbm, cot_hbm, weights_ref, out_ref, tokens_ref, cot_ref, q_cols, d_cols, norm_ref, pieces, got, near, far, load_sem, sum_send, sum_recv, near_send,
     near_recv, far_send, far_recv,
 ):
     blocks, queries, features = tokens_ref.shape
@@ -102,23 +101,17 @@
         for t in range(15)
     ]
 
-    w_query = weights_ref[:features, :]
-    w_query_t = transposed(w_query)
+    w_query_t = transposed(weights_ref[:features, :])
     w_out = weights_ref[features:, :]
-    w_out_t = transposed(w_out)
 
     def project_tokens(i, norm):
-        rows = tokens_ref[i]
-        q_rows[i] = dot(rows, w_query).astype(BF16)
-        cols = dot_nt(w_query_t, rows).astype(BF16)
+        cols = dot_nt(w_query_t, tokens_ref[i]).astype(BF16)
         q_cols[i] = cols
         wide = cols.astype(F32).reshape(HEADS, head_dim, queries)
         return jnp.maximum(norm, jnp.sum(wide * wide, axis=1))
 
     def project_grads(i, carry):
-        grads = cot_ref[i]
-        d_rows[i] = dot(grads, w_out_t).astype(BF16)
-        d_cols[i] = dot_nt(w_out, grads).astype(BF16)
+        d_cols[i] = dot_nt(w_out, cot_ref[i]).astype(BF16)
         return carry
 
     norm_ref[...] = lax.fori_loop(
@@ -166,11 +159,11 @@
         name="pool_exchange",
         out_shape=(
             jax.ShapeDtypeStruct((16 * rows, features), F32),
-            by_rows, by_rows, by_rows, by_cols, by_rows, by_cols,
+            by_rows, by_rows, by_cols, by_cols,
             jax.ShapeDtypeStruct((HEADS, queries), F32),
         ),
         in_specs=[hbm, hbm, vmem],
-        out_specs=(vmem,) * 8,
+        out_specs=(vmem,) * 6,
         scratch_shapes=[
             pltpu.VMEM((16, rows // 16, features), F32),
             pltpu.VMEM((15, rows // 16, features), F32),
@@ -180,7 +173,7 @@
             *[dma((15,))] * 6,
         ],
         compiler_params=pltpu.CompilerParams(
-            collective_id=0, has_side_effects=True, vmem_limit_bytes=40 * 1024 * 1024
+            collective_id=0, has_side_effects=True, vmem_limit_bytes=44 * 1024 * 1024
         ),
     )(tokens, cot, weights)
 
@@ -337,7 +330,7 @@
 
 
 def attend_kernel(
-    tokens_ref, cot_ref, pool_ref, q_rows, q_cols, d_rows, d_cols, norm_ref, w_key_ref,
+    tokens_ref, cot_ref, pool_ref, q_cols, d_cols, norm_ref, w_key_ref,
     w_value_ref, gain_ref, bias_ref, sums_ref, dq_ref, key_terms, value_terms, key_cols,
     value_cols, exps, dps, probs, dscores, key_sums, value_sums, attn_low, dq_low,
 ):
@@ -395,12 +388,12 @@
         dq_ref[i] = dq.astype(F32).T.astype(BF16)
 
     def keys_over_queries(i, h):
-        rows = pl.ds(h * keys, keys)
-        key_sums[rows, :] += dot(dscores[rows, :], q_rows[i])
+        head = pl.ds(h * head_dim, head_dim)
+        key_sums[head, :] += dot_nt(q_cols[i, head, :], dscores[pl.ds(h * keys, keys), :])
 
     def values_over_queries(i, h):
-        rows = pl.ds(h * keys, keys)
-        value_sums[rows, :] += dot(probs[rows, :], d_rows[i])
+        head = pl.ds(h * head_dim, head_dim)
+        value_sums[head, :] += dot_nt(d_cols[i, head, :], probs[pl.ds(h * keys, keys), :])
 
     def stage(i, h, sums, safe, only_first=False):
         following = (h + 1) % HEADS
@@ -466,14 +459,11 @@
         keys_over_queries(blocks - 1, h)
         values_over_queries(blocks - 1, h)
 
-    for start, wide in ((0, key_sums), (keys, value_sums)):
-        total = wide[pl.ds(0, keys), :]
-        for h in range(1, HEADS):
-            total = jnp.where(lane_group == h, wide[pl.ds(h * keys, keys), :], total)
-        sums_ref[pl.ds(start, keys), :] = total
-
-
-def attend(tokens, cot, pool_sums, q_rows, q_cols, d_rows, d_cols, norm, w_key, w_value, gain, bias):
+    sums_ref[pl.ds(0, keys), :] = key_sums[...].T
+    sums_ref[pl.ds(keys, keys), :] = value_sums[...].T
+
+
+def attend(tokens, cot, pool_sums, q_cols, d_cols, norm, w_key, w_value, gain, bias):
     blocks, queries, features = tokens.shape
     keys = pool_sums.shape[0]
     flops = 2 * blocks * queries * features * (6 * keys + 2 * features)
@@ -485,7 +475,7 @@
             jax.ShapeDtypeStruct((2 * keys + 2 * features, features), F32),
             jax.ShapeDtypeStruct((blocks, queries, features), BF16),
         ),
-        in_specs=[vmem] * 12,
+        in_specs=[vmem] * 10,
         out_specs=(vmem, vmem),
         scratch_shapes=[
             pltpu.VMEM((HEADS, keys, features), BF16),
@@ -496,8 +486,8 @@
             pltpu.VMEM((2, keys, queries), F32),
             pltpu.VMEM((HEADS * keys, queries), BF16),
             pltpu.VMEM((HEADS * keys, queries), BF16),
-            pltpu.VMEM((HEADS * keys, features), F32),
-            pltpu.VMEM((HEADS * keys, features), F32),
+            pltpu.VMEM((features, keys), F32),
+            pltpu.VMEM((features, keys), F32),
             pltpu.VMEM((features, queries), BF16),
             pltpu.VMEM((features, queries), BF16),
         ],
@@ -507,7 +497,7 @@
             transcendentals=blocks * queries * keys * HEADS,
         ),
         compiler_params=pltpu.CompilerParams(vmem_limit_bytes=28 * 1024 * 1024),
-    )(tokens, cot, pool_sums, q_rows, q_cols, d_rows, d_cols, norm, w_key, w_value, gain, bias)
+    )(tokens, cot, pool_sums, q_cols, d_cols, norm, w_key, w_value, gain, bias)
 
 
 def split_dot(low, wide):
@@ -605,13 +595,13 @@
     slab_rows = rows_y * plane_x
     gain, bias = ln_gain.reshape(1, features), ln_bias.reshape(1, features)
     blocks = slab_rows // QUERIES
-    pool_sums, token_rows, cot_rows, q_rows, q_cols, d_rows, d_cols, norm = exchange_pools(
+    pool_sums, token_rows, cot_rows, q_cols, d_cols, norm = exchange_pools(
         tokens.reshape(blocks, QUERIES, features),
         cotangent.reshape(blocks, QUERIES, features),
         jnp.concatenate([w_query, w_out], axis=0),
     )
     sums, dq = attend(
-        token_rows, cot_rows, pool_sums, q_rows, q_cols, d_rows, d_cols, norm, w_key, w_value,
+        token_rows, cot_rows, pool_sums, q_cols, d_cols, norm, w_key, w_value,
         gain, bias,
     )
     sums = sum_devices(sums)

time: 132 us -> 128 us (0.970)
  Pallas kernels: 130 us -> 126 us
    pallas_call x1, Pallas kernels: 73.7 us -> 69.7 us  [attend(): pl.pallas_call(attend_kernel, name='attend', out_shape=(jax.ShapeDtypeStr...]
where the time goes in v5:
time: 128 us
  Pallas kernels  126 us (98%)
    pallas_call x1, Pallas kernels, attend(): pl.pallas_call(attend_kernel, name='attend', out_shape=(jax.ShapeDtypeStr...  69.7 us
    pallas_call x1, Pallas kernels, exchange_pools(): pl.pallas_call(pool_kernel, name='pool_exchange', out_shape=(jax.ShapeDty...  28 us
    pallas_call x1, Pallas kernels, sum_devices(): pl.pallas_call(sum_kernel, name='sum_devices', out_shape=jax.ShapeDtypeSt...  25.3 us
    pallas_call x1, Pallas kernels, finish(): pl.pallas_call(functools.partial(finish_kernel, grad_scale), name='finish...  3.37 us

profile of v5, /device:TPU:1, one launch (start us, length us, event | category | flops | bytes accessed | tf_op | source)
XLA Modules:
  0.0 127.9 jit_solution(17251389842154099971)
XLA Ops:
  0.6 0.8 pad_maximum_fusion.weights_ref
  1.4 0.0 copy-start.1
  1.4 0.0 copy-start.2
  1.4 0.0 copy-start.3
  1.4 0.0 copy-start.4
  1.4 28.0 %pool_exchange.1 = (f32[512,128]{1,0:T(8,128)S(1)}, bf16[16,512,128]{2,1,0:T(8,128)(2,1)S(1)}, bf16[16,512,128]{2,1,0:T(8,128)(2,1)S(1)}, bf16[16,128,512]{2,1,0...) custom-call(bf16[16,512,128]{2,1,0:T(8,128)(2,1)} %bitcast.17, ...), custom_call_target="tpu_custom_call" | custom-call | tf_op jit(solution)/shard_map/pool_exchange/pallas_call | solution.py:157
  29.5 0.0 copy-done.1
  29.5 0.0 copy-done.2
  29.5 0.0 copy-done.3
  29.5 0.0 copy-done.4
  29.5 0.0 copy-start
  29.5 69.7 %attend.1 = (f32[1280,128]{1,0:T(8,128)S(1)}, bf16[16,512,128]{2,1,0:T(8,128)(2,1)S(1)}) custom-call(bf16[16,512,128]{2,1,0:T(8,128)(2,1)S(1)} %get-tuple-element.24.tokens_ref, bf16[16,512,128]{2,1,0:T(8,128)(2,1)S(1)} %get-tuple-element.25.cot_ref, f32[512,128]{1,0:T(8,128)S(1)} %get-tuple-element.26.pool_ref, ...), custom_call_target="tpu_custom_call" | custom-call | flops 6979321856 | bytes 6291456 | tf_op jit(solution)/shard_map/attend/pallas_call | solution.py:471
  99.3 25.3 %sum_devices.1 = f32[32,40,128]{2,1,0:T(8,128)S(1)} custom-call(f32[32,40,128]{2,1,0:T(8,128)S(1)} %bitcast.12), custom_call_target="tpu_custom_call" | custom-call | tf_op jit(solution)/shard_map/sum_devices/pallas_call | solution.py:276
  124.5 0.0 copy-done
  124.6 3.4 %finish.1 = (bf16[8192,128]{1,0:T(8,128)(2,1)}, f32[128,128]{1,0:T(8,128)}, f32[128,128]{1,0:T(8,128)}, f32[128,128]{1,0:T(8,128)}, f32[128,128]{1,0:T(8,128)}, ...) custom-call(f32[1280,128]{1,0:T(8,128)S(1)} %bitcast.10, f32[512,128]{1,0:T(8,128)S(1)} %get-tuple-element.26.pool_ref, ...), custom_call_target="tpu_custom_call" | custom-call | tf_op jit(solution)/shard_map/finish/pallas_call | solution.py:573
Async XLA Ops:
  1.4 28.1 %copy-start.1 = (bf16[128,128]{1,0:T(8,128)(2,1)S(1)}, bf16[128,128]{1,0:T(8,128)(2,1)}, u32[]{:S(2)}) copy-start(bf16[128,128]{1,0:T(8,128)(2,1)} %w_key_ref.3) | copy-start | bytes 98308
  1.4 28.1 %copy-start.2 = (bf16[128,128]{1,0:T(8,128)(2,1)S(1)}, bf16[128,128]{1,0:T(8,128)(2,1)}, u32[]{:S(2)}) copy-start(bf16[128,128]{1,0:T(8,128)(2,1)} %w_value_ref.3) | copy-start | bytes 98308
  1.4 28.1 %copy-start.3 = (f32[128]{0:T(128)S(1)}, f32[128]{0:T(128)}, u32[]{:S(2)}) copy-start(f32[128]{0:T(128)} %param.14) | copy-start | bytes 1540
  1.4 28.1 %copy-start.4 = (f32[128]{0:T(128)S(1)}, f32[128]{0:T(128)}, u32[]{:S(2)}) copy-start(f32[128]{0:T(128)} %param.15) | copy-start | bytes 1540
  29.5 95.0 %copy-start = (bf16[128,128]{1,0:T(8,128)(2,1)S(1)}, bf16[128,128]{1,0:T(8,128)(2,1)}, u32[]{:S(2)}) copy-start(bf16[128,128]{1,0:T(8,128)(2,1)} %w_query_ref.1) | copy-start | bytes 98308

commit v6 on v5

--- a/solution.py
+++ b/solution.py
@@ -17,7 +17,7 @@
 Z = 8
 PLANE = 16
 QUERIES = 512
-KEY_CHUNK = 256
+KEY_CHUNK = 512
 SAFE = 40.0
 
 
@@ -69,7 +69,7 @@
         for k, (source, target) in enumerate(((tokens_hbm, tokens_ref), (cot_hbm, cot_ref)))
         for n in range(LOADS)
     ]
-    for load in loads:
+    for load in loads[:LOADS]:
         load.start()
 
     me = lax.axis_index("gz")
@@ -95,6 +95,8 @@
         cells = jnp.sum(rows.reshape(cells_x, POOL, features), axis=1)
         for x in range(cells_x // share):
             pieces[y * (cells_x // share) + x] = cells[x * share : (x + 1) * share, :]
+    for load in loads[LOADS:]:
+        load.start()
     await_partners()
     copies = [
         send(pieces.at[members[t]], got.at[t], sum_send.at[t], sum_recv.at[t], near_ids[t])

time: 128 us -> 128 us (level)
  no operation moved by 1% of the time
where the time goes in v6:
time: 128 us
  Pallas kernels  126 us (98%)
    pallas_call x1, Pallas kernels, attend(): pl.pallas_call(attend_kernel, name='attend', out_shape=(jax.ShapeDtypeStr...  69.5 us
    pallas_call x1, Pallas kernels, exchange_pools(): pl.pallas_call(pool_kernel, name='pool_exchange', out_shape=(jax.ShapeDty...  28 us
    pallas_call x1, Pallas kernels, sum_devices(): pl.pallas_call(sum_kernel, name='sum_devices', out_shape=jax.ShapeDtypeSt...  25.3 us
    pallas_call x1, Pallas kernels, finish(): pl.pallas_call(functools.partial(finish_kernel, grad_scale), name='finish...  3.39 us

profile of v6, /device:TPU:1, one launch (start us, length us, event | category | flops | bytes accessed | tf_op | source)
XLA Modules:
  0.0 127.8 jit_solution(8651293684966802093)
XLA Ops:
  0.6 0.8 pad_maximum_fusion.weights_ref
  1.4 0.0 copy-start.1
  1.4 0.0 copy-start.2
  1.4 0.0 copy-start.3
  1.4 0.0 copy-start.4
  1.4 28.0 %pool_exchange.1 = (f32[512,128]{1,0:T(8,128)S(1)}, bf16[16,512,128]{2,1,0:T(8,128)(2,1)S(1)}, bf16[16,512,128]{2,1,0:T(8,128)(2,1)S(1)}, bf16[16,128,512]{2,1,0...) custom-call(bf16[16,512,128]{2,1,0:T(8,128)(2,1)} %bitcast.17, ...), custom_call_target="tpu_custom_call" | custom-call | tf_op jit(solution)/shard_map/pool_exchange/pallas_call | solution.py:159
  29.5 0.0 copy-done.1
  29.5 0.0 copy-done.2
  29.5 0.0 copy-done.3
  29.5 0.0 copy-done.4
  29.5 0.0 copy-start
  29.5 69.5 %attend.1 = (f32[1280,128]{1,0:T(8,128)S(1)}, bf16[16,512,128]{2,1,0:T(8,128)(2,1)S(1)}) custom-call(bf16[16,512,128]{2,1,0:T(8,128)(2,1)S(1)} %get-tuple-element.24.tokens_ref, bf16[16,512,128]{2,1,0:T(8,128)(2,1)S(1)} %get-tuple-element.25.cot_ref, f32[512,128]{1,0:T(8,128)S(1)} %get-tuple-element.26.pool_ref, ...), custom_call_target="tpu_custom_call" | custom-call | flops 6979321856 | bytes 6291456 | tf_op jit(solution)/shard_map/attend/pallas_call | solution.py:473
  99.1 25.3 %sum_devices.1 = f32[32,40,128]{2,1,0:T(8,128)S(1)} custom-call(f32[32,40,128]{2,1,0:T(8,128)S(1)} %bitcast.12), custom_call_target="tpu_custom_call" | custom-call | tf_op jit(solution)/shard_map/sum_devices/pallas_call | solution.py:278
  124.4 0.0 copy-done
  124.4 3.4 %finish.1 = (bf16[8192,128]{1,0:T(8,128)(2,1)}, f32[128,128]{1,0:T(8,128)}, f32[128,128]{1,0:T(8,128)}, f32[128,128]{1,0:T(8,128)}, f32[128,128]{1,0:T(8,128)}, ...) custom-call(f32[1280,128]{1,0:T(8,128)S(1)} %bitcast.10, f32[512,128]{1,0:T(8,128)S(1)} %get-tuple-element.26.pool_ref, ...), custom_call_target="tpu_custom_call" | custom-call | tf_op jit(solution)/shard_map/finish/pallas_call | solution.py:575
Async XLA Ops:
  1.4 28.1 %copy-start.1 = (bf16[128,128]{1,0:T(8,128)(2,1)S(1)}, bf16[128,128]{1,0:T(8,128)(2,1)}, u32[]{:S(2)}) copy-start(bf16[128,128]{1,0:T(8,128)(2,1)} %w_key_ref.3) | copy-start | bytes 98308
  1.4 28.1 %copy-start.2 = (bf16[128,128]{1,0:T(8,128)(2,1)S(1)}, bf16[128,128]{1,0:T(8,128)(2,1)}, u32[]{:S(2)}) copy-start(bf16[128,128]{1,0:T(8,128)(2,1)} %w_value_ref.3) | copy-start | bytes 98308
  1.4 28.1 %copy-start.3 = (f32[128]{0:T(128)S(1)}, f32[128]{0:T(128)}, u32[]{:S(2)}) copy-start(f32[128]{0:T(128)} %param.14) | copy-start | bytes 1540
  1.4 28.1 %copy-start.4 = (f32[128]{0:T(128)S(1)}, f32[128]{0:T(128)}, u32[]{:S(2)}) copy-start(f32[128]{0:T(128)} %param.15) | copy-start | bytes 1540
  29.5 94.8 %copy-start = (bf16[128,128]{1,0:T(8,128)(2,1)S(1)}, bf16[128,128]{1,0:T(8,128)(2,1)}, u32[]{:S(2)}) copy-start(bf16[128,128]{1,0:T(8,128)(2,1)} %w_query_ref.1) | copy-start | bytes 98308
